TPU v7x, 32 devices: a whole 2x2x4 slice. The times are simulated.
32 devices in a mesh: parts: 2 (over y), tensor: 16 (over z, x, core).
Axes of the slice: x: 2, y: 2, z: 4, core: 2. Of those that a mesh axis runs over, the one named last changes fastest.
Arguments:
- tokens: bfloat16 [32, 8192], P(('parts', 'tensor')), parts along dimension 0, may hold values from -6 to 6
- cotangent: bfloat16 [32, 8192], P(('parts', 'tensor')), parts along dimension 0, may hold values from -6 to 6
- token_adapter_index: int32 [32], P(('parts', 'tensor')), parts along dimension 0, may hold values from 0 to 63
- adapter_storage_slot: int32 [64], replicated, may hold values from 0 to 63, each once
- gate_weight: bfloat16 [8192, 16384], P(None, 'tensor'), may hold values from -0.0625 to 0.0625
- up_weight: bfloat16 [8192, 16384], P(None, 'tensor'), may hold values from -0.0625 to 0.0625
- down_weight: bfloat16 [16384, 8192], P('tensor'), may hold values from -0.046875 to 0.046875
- adapter_down_factors: bfloat16 [64, 16, 16384], P(None, None, 'tensor'), may hold values from -0.046875 to 0.046875
- adapter_up_factors: bfloat16 [64, 16, 8192], P('tensor'), may hold values from -1.5 to 1.5
Outputs:
- mixed: bfloat16 [32, 8192], P(('parts', 'tensor')), parts along dimension 0
- input_grad: bfloat16 [32, 8192], P(('parts', 'tensor')), parts along dimension 0
- down_grad: bfloat16 [128, 16, 16384], P('parts', None, 'tensor'), parts along dimension 0
- up_factor_gradient: bfloat16 [128, 16, 8192], P(('parts', 'tensor')), parts along dimension 0
There are 2 independent parts, one for each index of `parts`. A program takes and returns all parts, laid end to end along the dimension named above; an argument that names none is the same for every part. Nothing has to cross between parts.
Inputs may be any that keep to these rules, and one draw needn't show every extreme that they name: `adapter_storage_slot`: each slot once.
All inputs are finite; a program needn't handle non-finite values.
Results may differ from a plain program's by a relative error of at most 0.009.
Values may be sent and summed in bfloat16 or wider, within the bound.
No kernel may reach another device: no remote copies, remote signals or barrier semaphores. Data moves between devices by JAX's collectives and lax.ppermute only.
A program may use at most 128 MiB of HBM per device.

v0:
```python
import jax
import jax.numpy as jnp
from jax import lax
from jax.sharding import PartitionSpec as P

adapter_scale = 2.0


def per_device(
    tokens,
    cotangent,
    token_adapter_index,
    adapter_storage_slot,
    gate_weight,
    up_weight,
    down_weight,
    adapter_down_factors,
    adapter_up_factors,
):
    devices = lax.axis_size("tensor")
    my_index = lax.axis_index("tensor")
    tok_dev = tokens.shape[0]
    layer_width = tokens.shape[1]
    hidden_dev = gate_weight.shape[1]
    kept_factors = adapter_up_factors.shape[0]
    rank_values = adapter_up_factors.shape[1]
    count = adapter_storage_slot.shape[0]
    all_ids = lax.all_gather(token_adapter_index, "tensor", axis=0, tiled=True)
    table = jnp.arange(count, dtype=jnp.int32)
    storage_position = jnp.sum(
        jnp.where(all_ids[:, None] == table[None, :], adapter_storage_slot[None, :], 0), axis=1
    )
    owner = storage_position // kept_factors
    local = storage_position % kept_factors
    mine = owner == my_index
    select = (
        mine[:, None] & (local[:, None] == jnp.arange(kept_factors, dtype=jnp.int32)[None, :])
    ).astype(jnp.float32)
    total = select.shape[0]
    paired = jnp.concatenate((gate_weight, up_weight), axis=1)
    joined = jnp.dot(
        lax.all_gather(tokens, "tensor", axis=0, tiled=True),
        paired,
        preferred_element_type=jnp.float32,
    )
    gate = joined[:, :hidden_dev]
    up = joined[:, hidden_dev:]
    sig = jax.nn.sigmoid(gate)
    silu = gate * sig
    hidden_units_value = (silu * up).astype(jnp.bfloat16)
    down_factor_rows = adapter_down_factors[storage_position]
    rank_portion = jnp.einsum(
        "lb,lsb->ls", hidden_units_value, down_factor_rows, preferred_element_type=jnp.float32
    )
    rank_input = lax.psum(rank_portion, "tensor")
    up_factor_flattened = adapter_up_factors.reshape(kept_factors * rank_values, layer_width)
    rank_high = rank_input.astype(jnp.bfloat16)
    rank_low = (rank_input - rank_high.astype(jnp.float32)).astype(jnp.bfloat16)
    select_b = select.astype(jnp.bfloat16)
    weighted_high = (select_b[:, :, None] * rank_high[:, None, :]).reshape(
        total, kept_factors * rank_values
    )
    weighted_low = (select_b[:, :, None] * rank_low[:, None, :]).reshape(
        total, kept_factors * rank_values
    )
    adapted_total = jnp.dot(
        weighted_high, up_factor_flattened, preferred_element_type=jnp.float32
    ) + jnp.dot(weighted_low, up_factor_flattened, preferred_element_type=jnp.float32)
    adapted_output = (adapter_scale * adapted_total).astype(jnp.bfloat16)
    base = lax.psum_scatter(
        jnp.dot(hidden_units_value, down_weight, preferred_element_type=jnp.float32),
        "tensor",
        scatter_dimension=0,
        tiled=True,
    )
    returned = lax.all_to_all(
        adapted_output.reshape(devices, tok_dev, layer_width),
        "tensor",
        split_axis=0,
        concat_axis=0,
        tiled=True,
    )
    mixed = (base + jnp.sum(returned.astype(jnp.float32), axis=0)).astype(jnp.bfloat16)
    cot_all = lax.all_gather(cotangent, "tensor", axis=0, tiled=True)
    pulled = lax.dot_general(
        cot_all, up_factor_flattened, (((1,), (1,)), ((), ())), preferred_element_type=jnp.float32
    )
    rank_portion_output = adapter_scale * jnp.sum(
        select[:, :, None] * pulled.reshape(total, kept_factors, rank_values), axis=1
    )
    rank_output = lax.psum(rank_portion_output, "tensor").astype(jnp.bfloat16)
    contract = (((0,), (0,)), ((), ()))
    up_factor_total = lax.dot_general(
        weighted_high, cot_all, contract, preferred_element_type=jnp.float32
    ) + lax.dot_general(weighted_low, cot_all, contract, preferred_element_type=jnp.float32)
    up_factor_gradient = (
        (adapter_scale * up_factor_total)
        .reshape(kept_factors, rank_values, layer_width)
        .astype(jnp.bfloat16)
    )
    hidden_gradient = lax.dot_general(
        cot_all, down_weight, (((1,), (1,)), ((), ())), preferred_element_type=jnp.float32
    )
    hidden_gradient = hidden_gradient + jnp.einsum(
        "nz,nzu->nu", rank_output, down_factor_rows, preferred_element_type=jnp.float32
    )
    gate_grad = (hidden_gradient * up * sig * (1.0 + gate * (1.0 - sig))).astype(jnp.bfloat16)
    up_grad_h = (hidden_gradient * silu).astype(jnp.bfloat16)
    first = lax.dot_general(
        gate_grad, gate_weight, (((1,), (1,)), ((), ())), preferred_element_type=jnp.float32
    )
    second = lax.dot_general(
        up_grad_h, up_weight, (((1,), (1,)), ((), ())), preferred_element_type=jnp.float32
    )
    input_grad = lax.psum_scatter(first + second, "tensor", scatter_dimension=0, tiled=True).astype(
        jnp.bfloat16
    )
    onehot = (storage_position[None, :] == table[:, None]).astype(jnp.bfloat16)
    left = onehot[:, :, None] * rank_output[None, :, :]
    down_grad = jnp.einsum(
        "atr,tf->arf", left, hidden_units_value, preferred_element_type=jnp.float32
    ).astype(jnp.bfloat16)
    return (mixed, input_grad, down_grad, up_factor_gradient)


def solution(mesh):
    in_specs = (
        P(("parts", "tensor"), None),
        P(("parts", "tensor"), None),
        P(("parts", "tensor")),
        P(),
        P(None, "tensor"),
        P(None, "tensor"),
        P("tensor", None),
        P(None, None, "tensor"),
        P("tensor", None, None),
    )
    out_specs = (
        P(("parts", "tensor"), None),
        P(("parts", "tensor"), None),
        P("parts", None, "tensor"),
        P(("parts", "tensor"), None, None),
    )
    return jax.shard_map(
        per_device, mesh=mesh, in_specs=in_specs, out_specs=out_specs, check_vma=False
    )
```

profile of v0, /device:TPU:0, one launch (start us, length us, event | category | flops | bytes accessed | tf_op | source)
XLA Modules:
  0.0 331.8 jit_solution(16856081702424948918)
XLA Ops:
  7.2 0.0 copy-start
  8.0 1.4 fusion.45
  9.4 0.8 dynamic-update-slice
  10.1 13.7 %all-reduce = s32[16]{0:T(128)S(1)} all-reduce(s32[16]{0:T(128)S(1)} %dynamic-update-slice), channel_id=1, replica_groups=mesh['parts'=2,'tensor'=16] {'tensor'}, use_global_device_ids=true, to_apply=%add | all-reduce | flops 16 | bytes 128
  23.8 0.8 select_reduce_fusion
  24.7 0.5 copy-done.8
  25.2 19.6 %all-gather.1 = bf16[16,1,8192]{2,1,0:T(2,128)(2,1)S(1)} all-gather(bf16[1,1,8192]{2,1,0:T(2,128)(2,1)} %bitcast.63), channel_id=1, replica_groups=mesh['parts'=2,'tensor'=16] {'tensor'}, dimensions={0}, use_global_device_ids=true | all-gather | bytes 278528 | tf_op jit(solution)/shard_map/all_gather | solution.py:84
  44.8 0.3 copy.36
  45.1 0.6 fusion.44
  45.7 2.5 fusion.13
  48.2 31.1 %psum.15 = bf16[16,16]{1,0:T(8,128)(2,1)S(1)} all-reduce(f32[16,16]{1,0:T(8,128)S(1)} %broadcast_multiply_fusion.2), channel_id=1, replica_groups=mesh['parts'=2,'tensor'=16] {'tensor'}, use_global_device_ids=true, to_apply=%region_5.6 | all-reduce | flops 256 | bytes 1536 | tf_op jit(solution)/shard_map/psum | solution.py:91
  79.3 19.0 %all-gather = bf16[16,1,8192]{2,1,0:T(2,128)(2,1)S(1)} all-gather(bf16[1,1,8192]{2,1,0:T(2,128)(2,1)} %bitcast.64), channel_id=1, replica_groups=mesh['parts'=2,'tensor'=16] {'tensor'}, dimensions={0}, use_global_device_ids=true | all-gather | bytes 278528 | tf_op jit(solution)/shard_map/all_gather | solution.py:42
  98.4 12.2 %fusion.10 = f32[16,2048]{1,0:T(8,128)S(1)} fusion(bf16[8192,1024]{1,0:T(8,128)(2,1)} %param.14, bf16[8192,1024]{1,0:T(8,128)(2,1)} %param.13, bf16[16,1,8192]{2,1,0:T(2,128)(2,1)S(1)} %all-gather), kind=kOutput, calls=%fused_computation.15 | convolution fusion | flops 603979776 | bytes 33947648 | tf_op jit(solution)/shard_map/dot_general | solution.py:41
  110.6 0.6 fusion.59
  111.2 0.6 gather_fusion
  111.8 0.0 copy-start.2
  111.8 0.2 fusion.33
  112.0 0.6 copy-done.2
  112.6 10.2 %convolution_add_fusion.2 = f32[16,1024]{1,0:T(8,128)S(1)} fusion(bf16[1024,8192]{1,0:T(8,128)(2,1)} %param.15, bf16[16,1,8192]{2,0,1:T(8,128)(2,1)S(1)} %copy.36, f32[16,1,1024]{2,1,0:T(1,128)S(1)} %fusion.33), kind=kOutput, calls=%fused_computation.17 | convolution fusion | flops 268451840 | bytes 17170432 | tf_op jit(solution)/shard_map/dot_general | solution.py:101
  122.8 0.0 copy-start.1
  122.8 10.3 %fusion.27 = f32[16,8192]{1,0:T(8,128)S(1)} fusion(bf16[8192,1024]{1,0:T(8,128)(2,1)} %param.13, f32[16,1024]{1,0:T(8,128)S(1)} %convolution_add_fusion.2, f32[16,2048]{1,0:T(8,128)S(1)} %fusion.10), kind=kOutput, calls=%fused_computation.38 | convolution fusion | flops 268599296 | bytes 17498112 | tf_op jit(solution)/shard_map/dot_general | solution.py:109
  133.1 11.2 %convolution_add_fusion.1 = f32[16,8192]{1,0:T(8,128)} fusion(f32[16,8192]{1,0:T(8,128)S(1)} %fusion.27, bf16[8192,1024]{1,0:T(8,128)(2,1)} %param.14, f32[16,1024]{1,0:T(8,128)S(1)} %convolution_add_fusion.2, f32[16,2048]{1,0:T(8,128)S(1)} %fusion.10), kind=kOutput, calls=%fused_computation.8 | convolution fusion | flops 268664832 | bytes 17956864 | tf_op jit(solution)/shard_map/dot_general | solution.py:112
  144.4 0.3 fusion.24
  144.7 66.4 %all-reduce.8 = (f32[16,16]{1,0:T(8,128)S(1)}, bf16[16,8192]{1,0:T(8,128)(2,1)}) all-reduce(f32[16,16]{1,0:T(8,128)S(1)} %bitcast.65, f32[16,8192]{1,0:T(8,128)} %convolution_add_fusion.1), channel_id=1, replica_groups=mesh['parts'=2,'tensor'=16] {'tensor'}, use_global_device_ids=true, to_apply=%region_2.3 | all-reduce | flops 131328 | bytes 788480 | tf_op jit(solution)/shard_map/psum | solution.py:55
  211.0 0.6 subtract_convert_fusion
  211.6 1.3 copy.26
  212.9 0.8 broadcast_multiply_fusion.1
  213.8 0.5 convolution_bitcast_fusion
  214.2 0.1 copy-done.4
  214.4 1.2 fusion.9
  215.5 0.5 broadcast.185
  216.1 1.8 reduce.1
  217.8 0.9 reshape.190
  218.7 3.5 %all-to-all-start = ((bf16[16,2,4096]{2,1,0:T(2,128)(2,1)}), bf16[16,2,4096]{2,1,0:T(2,128)(2,1)S(1)}, u32[]{:S(2)}, u32[]{:S(2)}) async-start(bf16[16,2,4096]{2,1,0:T(2,128)(2,1)} %reshape.190), calls=%async_computation | async-start | bytes 524288 | tf_op jit(solution)/shard_map/all_to_all | solution.py:76
  222.3 0.0 all-reduce.7.cloned.1.call-start
  222.3 8.9 %fusion.46 = f32[16,8192]{1,0:T(8,128)} fusion(bf16[16,1024]{1,0:T(8,128)(2,1)S(1)} %multiply_convert_fusion.2, bf16[1024,8192]{1,0:T(8,128)(2,1)} %param.15), kind=kOutput, calls=%fused_computation.73 | convolution fusion | flops 268435456 | bytes 17334272 | tf_op jit(solution)/shard_map/dot_general | solution.py:71
  231.2 0.0 all-reduce.7.cloned.1.call-update
  231.3 0.1 mul.113
  231.4 0.1 mul.114
  231.4 0.8 copy.30
  232.2 0.4 fusion.15
  232.6 1.4 fusion.5
  234.1 2.2 dynamic-slice_convert_fusion
  236.3 2.0 convolution_convert_fusion
  238.3 0.3 reshape.191
  238.6 0.6 convert_reduce_fusion
  239.2 83.5 %all-reduce.7.cloned.1.call-done = f32[16,8192]{1,0:T(8,128)} async-done(((f32[16,8192]{1,0:T(8,128)}), f32[16,8192]{1,0:T(8,128)}) %all-reduce.7.cloned.1.call-update) | async-done | bytes 524304
  322.7 2.2 fusion.28
  (23 shorter events, 0.1 us)
Async XLA Ops:
  7.2 104.0 %copy-start = (bf16[64,16,1024]{2,1,0:T(8,128)(2,1)S(1)}, bf16[64,16,1024]{2,1,0:T(8,128)(2,1)}, u32[]{:S(2)}) copy-start(bf16[64,16,1024]{2,1,0:T(8,128)(2,1)} %param.16) | copy-start | bytes 6291460
  24.7 0.5 copy-start.8
  79.3 32.5 %copy-start.6 = (bf16[16,16]{1,0:T(8,128)(2,1)}, bf16[16,16]{1,0:T(8,128)(2,1)S(1)}, u32[]{:S(2)}) copy-start(bf16[16,16]{1,0:T(8,128)(2,1)S(1)} %psum.15) | copy-start | bytes 1540
  111.8 0.8 copy-start.2
  122.8 21.6 %copy-start.3 = (bf16[16,16,1024]{2,1,0:T(8,128)(2,1)S(1)}, bf16[16,16,1024]{2,1,0:T(8,128)(2,1)}, u32[]{:S(2)}) copy-start(bf16[16,16,1024]{2,1,0:T(8,128)(2,1)} %copy-done.2) | copy-start | bytes 1572868
  122.8 21.6 %copy-start.7 = (bf16[16,1024,1]{1,0,2:T(8,128)(2,1)S(1)}, bf16[16,1024,1]{1,0,2:T(8,128)(2,1)}, u32[]{:S(2)}) copy-start(bf16[16,1024,1]{1,0,2:T(8,128)(2,1)} %fusion.59) | copy-start | bytes 98308
  122.8 91.0 %copy-start.1 = (bf16[4,16,8192]{2,1,0:T(8,128)(2,1)S(1)}, bf16[4,16,8192]{2,1,0:T(8,128)(2,1)}, u32[]{:S(2)}) copy-start(bf16[4,16,8192]{2,1,0:T(8,128)(2,1)} %param.17) | copy-start | bytes 3145732
  213.7 0.6 copy-start.4
  215.5 15.7 %copy-start.5 = (bf16[16,4,16]{2,1,0:T(4,128)(2,1)S(1)}, bf16[16,4,16]{2,1,0:T(4,128)(2,1)}, u32[]{:S(2)}) copy-start(bf16[16,4,16]{2,1,0:T(4,128)(2,1)} %copy-done.4) | copy-start | bytes 6148
  215.5 20.7 %copy-start.9 = (s32[16]{0:T(128)S(1)}, s32[16]{0:T(128)}, u32[]{:S(2)}) copy-start(s32[16]{0:T(128)} %copy-done.8) | copy-start | bytes 196
  218.7 19.6 %all-to-all-start = ((bf16[16,2,4096]{2,1,0:T(2,128)(2,1)}), bf16[16,2,4096]{2,1,0:T(2,128)(2,1)S(1)}, u32[]{:S(2)}, u32[]{:S(2)}) async-start(bf16[16,2,4096]{2,1,0:T(2,128)(2,1)} %reshape.190), calls=%async_computation | async-start | bytes 524288 | tf_op jit(solution)/shard_map/all_to_all | solution.py:76
  222.3 100.4 %all-reduce.7.cloned.1.call-start = ((), (), s32[]{:S(2)}) async-start(), calls=%async_computation.1 | async-start | bytes 1048576
Sparse Core Ops, SparseCore 0:
  231.4 91.2 all-reduce.6
where the time goes:
time: 333 us; the launch traced here: 332 us
  blocking collectives  150 us (45%)
  waiting for transfers between devices  83.5 us (25%)
  matrix products  61.4 us (18%)
  between operations  15 us (5%)
  local copies, waits for them, and re-layouts  10.3 us (3%)
  other arithmetic  8.11 us (2%)
  starting transfers between devices  3.57 us (1%)
    unnamed x2, waiting for transfers between devices  83.5 us
    psum x1, blocking collectives, per_device(): rank_input = lax.psum(rank_portion, 'tensor')  66.4 us
    psum x1, blocking collectives, per_device(): rank_output = lax.psum(rank_portion_output, 'tensor').astype(jnp.bfloat16)  31.1 us
    all_gather x1, blocking collectives, per_device(): cot_all = lax.all_gather(cotangent, 'tensor', axis=0, tiled=True)  19.6 us
    all_gather x1, blocking collectives, per_device(): lax.all_gather(tokens, 'tensor', axis=0, tiled=True)  19 us
    unnamed x1, blocking collectives  13.7 us
    dot_general x1, matrix products, per_device(): jnp.dot(lax.all_gather(tokens, 'tensor', axis=0, tiled=True), paired, pre...  12.2 us
    dot_general x1, matrix products, per_device(): lax.dot_general(up_grad_h, up_weight, (((1,), (1,)), ((), ())), preferred...  11.2 us
  transfers between devices with their start and end apart: 2, of which 1 were waited for; matrix products, arithmetic and copies ran while one was open for 5% of the time, Pallas kernels for 0%

commit v1 on v0

v1 whole, which is shorter than its diff:
```python
import functools

import jax
import jax.numpy as jnp
from jax import lax
from jax.experimental import pallas as pl
from jax.experimental.pallas import tpu as pltpu
from jax.sharding import PartitionSpec as P

adapter_scale = 2.0
f32 = jnp.float32
bf16 = jnp.bfloat16
SPLIT = 128
VMEM = pl.BlockSpec(memory_space=pltpu.VMEM)
NT = (((1,), (1,)), ((), ()))
TN = (((0,), (0,)), ((), ()))


def params(mib):
    return pltpu.CompilerParams(vmem_limit_bytes=mib << 20)


def fit(size, want):
    return want if size % want == 0 else size


def slot_mask(slot, first, columns, rank):
    col = lax.broadcasted_iota(jnp.int32, (slot.shape[0], columns), 1) // rank
    return slot.astype(jnp.int32) == col + first


def fold_matrix(columns, rank, by_row):
    shape = (columns, rank) if by_row else (rank, columns)
    c = lax.broadcasted_iota(jnp.int32, shape, 0 if by_row else 1)
    r = lax.broadcasted_iota(jnp.int32, shape, 1 if by_row else 0)
    return jnp.where(c % rank == r, 1.0, 0.0).astype(bf16)


def halves(v):
    high = v.astype(bf16)
    return high, (v - high.astype(f32)).astype(bf16)


def dot(a, b, dims=(((1,), (0,)), ((), ()))):
    return lax.dot_general(a, b, dims, preferred_element_type=f32)


def dot2(v, b, dims=(((1,), (0,)), ((), ()))):
    high, low = halves(v)
    return dot(high, b, dims) + dot(low, b, dims)


def forward_kernel(
    x_ref, c_ref, slot_ref, wg_ref, wu_ref, d_ref, u_ref, gate_ref, up_ref, hid_ref, pay_ref
):
    total, width = x_ref.shape
    hidden_dev = wg_ref.shape[1]
    chunk = fit(width, 2048)
    half = total // 2

    def body(i, acc):
        s = pl.ds(pl.multiple_of(i * chunk, chunk), chunk)
        xs = x_ref[:, s]
        return acc[0] + dot(xs, wg_ref[s, :]), acc[1] + dot(xs, wu_ref[s, :])

    zero = jnp.zeros((total, hidden_dev), f32)
    gate, up = lax.fori_loop(0, width // chunk, body, (zero, zero))
    gate_ref[...] = gate
    up_ref[...] = up
    hid = (gate * jax.nn.sigmoid(gate) * up).astype(bf16)
    hid_ref[...] = hid
    rank = pay_ref.shape[1] // 4
    slot = slot_ref[...]
    columns = d_ref.shape[0]
    met = dot(hid, d_ref[...], NT)
    met = jnp.where(slot_mask(slot, 0, columns, rank), met, 0.0)
    rank_in = dot2(met, fold_matrix(columns, rank, True))
    kept = u_ref.shape[0]
    first = lax.axis_index("tensor") * (kept // rank)
    pulled = dot(c_ref[...], u_ref[...], NT)
    pulled = jnp.where(slot_mask(slot, first, kept, rank), pulled, 0.0)
    rank_out = adapter_scale * dot2(pulled, fold_matrix(kept, rank, True))
    both = jnp.concatenate((rank_in, rank_out), axis=1)
    swap = lax.axis_index("tensor") % 2
    own, sib = both[:half], both[half:]
    pay_ref[...] = jnp.concatenate(
        (jnp.where(swap == 0, own, sib), jnp.where(swap == 0, sib, own)), axis=1
    )


def down_kernel(hid_ref, c_ref, wd_ref, base_ref, pull_ref):
    width = wd_ref.shape[1]
    hidden_dev = wd_ref.shape[0]
    chunk = fit(width, 1024)

    def body(i, _):
        s = pl.ds(pl.multiple_of(i * chunk, chunk), chunk)
        base_ref[:, s] = dot(hid_ref[...], wd_ref[:, s])
        return 0

    lax.fori_loop(0, width // chunk, body, 0)
    rows = fit(hidden_dev, 256)

    def body2(i, _):
        s = pl.ds(pl.multiple_of(i * rows, rows), rows)
        pull_ref[:, s] = dot(c_ref[...], wd_ref[s, :], NT)
        return 0

    lax.fori_loop(0, hidden_dev // rows, body2, 0)


def backward_kernel(
    got_ref, slot_ref, gate_ref, up_ref, base_ref, pull_ref, wg_ref, wu_ref, d_ref, u_ref,
    own_ref, sib_ref, left_ref, weighted_ref,
):
    total, hidden_dev = gate_ref.shape
    width = wg_ref.shape[0]
    half = total // 2
    rank = got_ref.shape[2] // 4
    columns = d_ref.shape[0]
    kept = u_ref.shape[0]
    got = jnp.sum(got_ref[...], axis=0)
    swap = lax.axis_index("tensor") % 2
    a, b = got[:, : 2 * rank], got[:, 2 * rank :]
    both = jnp.concatenate(
        (jnp.where(swap == 0, a, b), jnp.where(swap == 0, b, a)), axis=0
    )
    rank_in = both[:, :rank]
    rank_out = both[:, rank:].astype(bf16)
    slot = slot_ref[...]
    spread = dot(rank_out, fold_matrix(columns, rank, False))
    left = jnp.where(slot_mask(slot, 0, columns, rank), spread, 0.0).astype(bf16)
    left_ref[...] = left
    grad = pull_ref[...] + dot(left, d_ref[...])
    gate = gate_ref[...]
    up = up_ref[...]
    sig = jax.nn.sigmoid(gate)
    gg = (grad * up * sig * (1.0 + gate * (1.0 - sig))).astype(bf16)
    gu = (grad * (gate * sig)).astype(bf16)
    first = lax.axis_index("tensor") * (kept // rank)
    mine = slot_mask(slot, first, kept, rank)
    high, low = halves(rank_in)
    fold = fold_matrix(kept, rank, False)
    high = jnp.where(mine, dot(high, fold), 0.0).astype(bf16)
    low = jnp.where(mine, dot(low, fold), 0.0).astype(bf16)
    weighted = jnp.concatenate((high, low), axis=0)
    weighted_ref[...] = weighted
    chunk = fit(width, 1024)

    def body(i, _):
        s = pl.ds(pl.multiple_of(i * chunk, chunk), chunk)
        us = u_ref[:, s]
        adapted = adapter_scale * (dot(high, us) + dot(low, us))
        out = base_ref[:, s] + adapted.astype(bf16).astype(f32)
        inp = dot(gg, wg_ref[s, :], NT) + dot(gu, wu_ref[s, :], NT)
        own_ref[0, :, s] = out[:half]
        own_ref[1, :, s] = inp[:half]
        sib_ref[0, :, s] = out[half:].astype(bf16)
        sib_ref[1, :, s] = inp[half:].astype(bf16)
        return 0

    lax.fori_loop(0, width // chunk, body, 0)


def factor_kernel(left_ref, hid_ref, weighted_ref, c_ref, down_ref, upg_ref):
    columns = down_ref.shape[0]
    rows = fit(columns, 256)
    for i in range(columns // rows):
        s = pl.ds(i * rows, rows)
        down_ref[s, :] = dot(left_ref[:, s], hid_ref[...], TN).astype(bf16)
    width = c_ref.shape[1]
    chunk = fit(width, 1024)
    total = c_ref.shape[0]
    for i in range(width // chunk):
        s = pl.ds(i * chunk, chunk)
        cs = c_ref[:, s]
        both = dot(weighted_ref[:total], cs, TN) + dot(weighted_ref[total:], cs, TN)
        upg_ref[:, s] = (adapter_scale * both).astype(bf16)


def call(kernel, args, outs, mib, flops=0, nbytes=0):
    return pl.pallas_call(
        kernel,
        in_specs=[VMEM] * len(args),
        out_specs=[VMEM] * len(outs),
        out_shape=[jax.ShapeDtypeStruct(s, t) for s, t in outs],
        compiler_params=params(mib),
        cost_estimate=pl.CostEstimate(flops=flops, bytes_accessed=nbytes, transcendentals=0),
    )(*args)


def per_device(
    tokens,
    cotangent,
    token_adapter_index,
    adapter_storage_slot,
    gate_weight,
    up_weight,
    down_weight,
    adapter_down_factors,
    adapter_up_factors,
):
    devices = lax.axis_size("tensor")
    chips = devices // 2
    tok_dev, width = tokens.shape
    hidden_dev = gate_weight.shape[1]
    kept, rank = adapter_up_factors.shape[:2]
    count = adapter_storage_slot.shape[0]
    half = chips * tok_dev
    total = 2 * half
    room = 8 + total // 4
    same_core = [[c + 2 * i for i in range(chips)] for c in range(2)]
    pairs = [(i, i ^ 1) for i in range(devices)]

    wg, wu, wd = (
        pltpu.with_memory_space_constraint(w, pltpu.VMEM)
        for w in (gate_weight, up_weight, down_weight)
    )
    d = pltpu.with_memory_space_constraint(
        adapter_down_factors.reshape(count * rank, hidden_dev), pltpu.VMEM
    )
    u = pltpu.with_memory_space_constraint(
        adapter_up_factors.reshape(kept * rank, width), pltpu.VMEM
    )

    table = jnp.arange(count, dtype=jnp.int32)
    slot = jnp.sum(
        jnp.where(token_adapter_index[:, None] == table[None, :], adapter_storage_slot[None, :], 0),
        axis=1,
    )
    lanes = jnp.arange(SPLIT, dtype=jnp.int32)[None, :]
    digits = jnp.where(
        lanes == 0, slot[:, None] // SPLIT, jnp.where(lanes == 1, slot[:, None] % SPLIT, 0)
    ).astype(bf16)
    row = jnp.stack(
        (
            jnp.concatenate((tokens, digits), axis=1),
            jnp.concatenate((cotangent, jnp.zeros_like(digits)), axis=1),
        ),
        axis=1,
    )
    sent = jnp.broadcast_to(row[None], (chips,) + row.shape)
    own = lax.all_to_all(sent, "tensor", 0, 0, axis_index_groups=same_core, tiled=True)
    sib = lax.ppermute(own, "tensor", pairs)
    gathered = jnp.concatenate((own, sib), axis=0).reshape(total, 2, width + SPLIT)
    x = gathered[:, 0, :width]
    c = gathered[:, 1, :width]
    code = gathered[:, 0, width : width + 2].astype(f32)
    slots = code[:, 0:1] * SPLIT + code[:, 1:2]

    gate, up, hid, pay = call(
        forward_kernel,
        (x, c, slots, wg, wu, d, u),
        (
            ((total, hidden_dev), f32),
            ((total, hidden_dev), f32),
            ((total, hidden_dev), bf16),
            ((half, 4 * rank), f32),
        ),
        room,
    )
    got = lax.all_to_all(
        jnp.broadcast_to(pay[None], (devices,) + pay.shape), "tensor", 0, 0, tiled=True
    )
    base, pull = call(
        down_kernel,
        (hid, c, wd),
        (((total, width), f32), ((total, hidden_dev), f32)),
        room,
        flops=4 * total * width * hidden_dev,
        nbytes=2 * width * hidden_dev,
    )
    mine, theirs, left, weighted = call(
        backward_kernel,
        (got, slots, gate, up, base, pull, wg, wu, d, u),
        (
            ((2, half, width), f32),
            ((2, half, width), bf16),
            ((total, count * rank), bf16),
            ((2 * total, kept * rank), bf16),
        ),
        room,
    )
    summed = mine + lax.ppermute(theirs, "tensor", pairs).astype(f32)
    summed = jnp.transpose(
        summed.astype(bf16).reshape(2, chips, tok_dev, width), (1, 0, 2, 3)
    ).reshape(chips, 2 * tok_dev, width)
    back = lax.all_to_all(summed, "tensor", 0, 0, axis_index_groups=same_core, tiled=True)
    down_grad, up_factor_gradient = call(
        factor_kernel,
        (left, hid, weighted, c),
        (((count * rank, hidden_dev), bf16), ((kept * rank, width), bf16)),
        room,
        flops=2 * total * count * rank * hidden_dev,
        nbytes=2 * (count * rank * hidden_dev + kept * rank * width),
    )
    final = jnp.sum(back.astype(f32).reshape(chips, 2, tok_dev, width), axis=0).astype(bf16)
    return (
        final[0],
        final[1],
        down_grad.reshape(count, rank, hidden_dev),
        up_factor_gradient.reshape(kept, rank, width),
    )


def solution(mesh):
    in_specs = (
        P(("parts", "tensor"), None),
        P(("parts", "tensor"), None),
        P(("parts", "tensor")),
        P(),
        P(None, "tensor"),
        P(None, "tensor"),
        P("tensor", None),
        P(None, None, "tensor"),
        P("tensor", None, None),
    )
    out_specs = (
        P(("parts", "tensor"), None),
        P(("parts", "tensor"), None),
        P("parts", None, "tensor"),
        P(("parts", "tensor"), None, None),
    )
    return jax.shard_map(
        per_device, mesh=mesh, in_specs=in_specs, out_specs=out_specs, check_vma=False
    )
```

time: 333 us -> 111 us (0.33)
  blocking collectives: 150 us -> 16.9 us
  waiting for transfers between devices: 83.5 us -> 9.28 us
  matrix products: 61.4 us -> 0 us
  local copies, waits for them, and re-layouts: 10.3 us -> 39.1 us
  Pallas kernels: 0 us -> 27.4 us
  between operations: 15 us -> 4.18 us
  starting transfers between devices: 3.57 us -> 9.75 us
  other arithmetic: 8.11 us -> 3.51 us
    psum x2 -> x0, blocking collectives: 97.4 us -> none  [the longest x1 66.4 us: per_device(): rank_input = lax.psum(rank_portion, 'tensor')]
    unnamed x2 -> x0, waiting for transfers between devices: 83.5 us -> none
    dot_general x13 -> x0, matrix products: 61.4 us -> none  [the longest x1 12.2 us: per_device(): jnp.dot(lax.all_gather(tokens, 'tensor', axis=0, tiled=True), paired, pre...]
    all_gather x2 -> x0, blocking collectives: 38.7 us -> none  [the longest x1 19.6 us: per_device(): cot_all = lax.all_gather(cotangent, 'tensor', axis=0, tiled=True)]
    unnamed x26 -> x32, local copies, waits for them, and re-layouts: 4.81 us -> 36.1 us
    pallas_call x0 -> x4, Pallas kernels: none -> 27.4 us  [call(): pl.pallas_call(kernel, in_specs=[VMEM] * len(args), out_specs=[VMEM] * le...]
    all_to_all x0 -> x1, blocking collectives: none -> 16.9 us  [per_device(): lax.all_to_all(sent, 'tensor', 0, 0, axis_index_groups=same_core, tiled=T...]
    unnamed x1 -> x0, blocking collectives: 13.7 us -> none
  transfers between devices with their start and end apart: 2 -> 4, of which waited for: 1 -> 3; matrix products, arithmetic and copies ran while one was open for 5% -> 0% of each run, Pallas kernels for 0% -> 10%
where the time goes in v1:
time: 111 us; the launch traced here: 110 us
  local copies, waits for them, and re-layouts  39.1 us (35%)
  Pallas kernels  27.4 us (25%)
  blocking collectives  16.9 us (15%)
  starting transfers between devices  9.75 us (9%)
  waiting for transfers between devices  9.28 us (8%)
  between operations  4.18 us (4%)
  other arithmetic  3.51 us (3%)
    unnamed x32, local copies, waits for them, and re-layouts  36.1 us
    pallas_call x4, Pallas kernels, call(): pl.pallas_call(kernel, in_specs=[VMEM] * len(args), out_specs=[VMEM] * le...  27.4 us
    all_to_all x1, blocking collectives, per_device(): lax.all_to_all(sent, 'tensor', 0, 0, axis_index_groups=same_core, tiled=T...  16.9 us
    all_to_all x1, waiting for transfers between devices, per_device(): lax.all_to_all(summed, 'tensor', 0, 0, axis_index_groups=same_core, tiled...  6.5 us
    all_to_all x1, starting transfers between devices, per_device(): lax.all_to_all(summed, 'tensor', 0, 0, axis_index_groups=same_core, tiled...  5.87 us
    all_to_all x1, starting transfers between devices, per_device(): lax.all_to_all(jnp.broadcast_to(pay[None], (devices,) + pay.shape), 'tens...  3.5 us
  transfers between devices with their start and end apart: 4, of which 3 were waited for; matrix products, arithmetic and copies ran while one was open for 0% of the time, Pallas kernels for 10%

profile of v1, /device:TPU:0, one launch (start us, length us, event | category | flops | bytes accessed | tf_op | source)
XLA Modules:
  0.0 110.1 jit_solution(1752577963285968565)
XLA Ops:
  0.6 0.0 copy-start.6
  0.6 0.0 copy-start.5
  1.4 1.4 %fusion.3 = s32[]{:T(128)} fusion(s32[64]{0:T(128)} %param.12, s32[]{:T(128)} %bitcast.31), kind=kLoop, calls=%fused_computation.16 | loop fusion | flops 191 | bytes 264 | tf_op jit(solution)/shard_map/reduce_sum | solution.py:227
  5.5 0.8 maximum_bitcast_fusion.1
  6.4 0.1 maximum_bitcast_fusion.2
  6.5 0.1 broadcast_in_dim.56
  6.6 16.9 %all_to_all.15 = bf16[8,1,2,8320]{3,2,1,0:T(2,128)(2,1)S(1)} all-to-all(bf16[8,1,2,8320]{3,2,1,0:T(2,128)(2,1)S(1)} %broadcast_in_dim.56), channel_id=1, replica_groups={{0,2,4,6,8,10,12,14},{1,3,5,7,9,11,13,15},{16,18,20,22,24,26,28,30},{17..., dimensions={0} | all-to-all | bytes 532480 | tf_op jit(solution)/shard_map/all_to_all | solution.py:243
  23.5 0.1 collective-permute-start
  23.6 1.5 %collective-permute-done = bf16[8,1,2,8320]{3,0,2,1:T(8,128)(2,1)S(1)} collective-permute-done((bf16[8,1,2,8320]{3,0,2,1:T(8,128)(2,1)S(1)}, bf16[8,1,2,8320]{3,0,2,1:T(8,128)(2,1)S(1)}, u32[]{:S(2)}, u32[]{:S(2)}) %collective-permute-start) | collective-permute-done | bytes 266272 | tf_op jit(solution)/shard_map/ppermute | solution.py:244
  25.2 0.1 slice_add_fusion.slot_ref
  25.3 0.0 copy-done.6
  25.3 0.0 copy-done.5
  25.3 0.0 copy-start
  25.3 5.8 %copy-done = bf16[8192,1024]{1,0:T(8,128)(2,1)S(1)} copy-done((bf16[8192,1024]{1,0:T(8,128)(2,1)S(1)}, bf16[8192,1024]{1,0:T(8,128)(2,1)}, u32[]{:S(2)}) %copy-start) | copy-done | bytes 16777240
  31.1 0.0 copy-start.2
  31.1 5.8 %copy-done.2 = bf16[8192,1024]{1,0:T(8,128)(2,1)S(1)} copy-done((bf16[8192,1024]{1,0:T(8,128)(2,1)S(1)}, bf16[8192,1024]{1,0:T(8,128)(2,1)}, u32[]{:S(2)}) %copy-start.2) | copy-done | bytes 16777240
  36.8 6.2 %shard_map.120 = (f32[16,1024]{1,0:T(8,128)S(1)}, f32[16,1024]{1,0:T(8,128)S(1)}, bf16[16,1024]{1,0:T(8,128)(2,1)S(1)}, f32[8,64]{1,0:T(8,128)S(1)}) custom-call(bf16[16,8192]{1,0:T(8,128)(2,1)S(1)} %get-tuple-element.29.x_ref, bf16[16,8192]{1,0:T(8,128)(2,1)S(1)} %get-tuple-element.28.c_ref, f32[16,1]{1,0:T(8,128)S(1)} %slice_add_fusion.slot_ref, ...), custom_call_target="tpu_custom_call" | custom-call | tf_op jit(solution)/shard_map/pallas_call | solution.py:182
  43.0 0.0 copy-start.11
  43.0 0.7 copy-done.11
  43.6 0.6 broadcast_in_dim.57
  44.3 1.6 %reshape.102 = f32[16,1,512]{2,1,0:T(1,128)} reshape(f32[16,8,64]{2,1,0:T(8,128)} %broadcast_in_dim.57) | data formatting | bytes 65536
  45.8 3.5 %all-to-all-start.1 = ((f32[16,1,512]{2,1,0:T(1,128)}), f32[16,1,512]{2,1,0:T(1,128)S(1)}, u32[]{:S(2)}, u32[]{:S(2)}) async-start(f32[16,1,512]{2,1,0:T(1,128)} %reshape.102), calls=%async_computation.1 | async-start | bytes 65536 | tf_op jit(solution)/shard_map/all_to_all | solution.py:262
  49.3 0.0 copy-start.4
  49.4 5.8 %copy-done.4 = bf16[1024,8192]{1,0:T(8,128)(2,1)S(1)} copy-done((bf16[1024,8192]{1,0:T(8,128)(2,1)S(1)}, bf16[1024,8192]{1,0:T(8,128)(2,1)}, u32[]{:S(2)}) %copy-start.4) | copy-done | bytes 16777240
  55.1 7.9 %shard_map.121 = (f32[16,8192]{1,0:T(8,128)S(1)}, f32[16,1024]{1,0:T(8,128)S(1)}) custom-call(bf16[16,1024]{1,0:T(8,128)(2,1)S(1)} %get-tuple-element.19.hid_ref, bf16[16,8192]{1,0:T(8,128)(2,1)S(1)} %get-tuple-element.28.c_ref, bf16[1024,8192]{1,0:T(8,128)(2,1)S(1)} %copy-done.4), custom_call_target="tpu_custom_call" | custom-call | flops 536870912 | bytes 16777216 | tf_op jit(solution)/shard_map/pallas_call | solution.py:182
  63.0 0.0 copy-done.9
  63.0 0.8 copy-done.7
  63.8 0.6 copy-done.13
  64.4 0.0 all-to-all-done.1
  64.4 0.5 broadcast.58
  65.0 0.7 reduce.5
  65.7 0.1 reshape.103.got_ref
  65.8 5.8 %copy-done.1 = bf16[8192,1024]{1,0:T(8,128)(2,1)S(1)} copy-done((bf16[8192,1024]{1,0:T(8,128)(2,1)S(1)}, bf16[8192,1024]{1,0:T(8,128)(2,1)}, u32[]{:S(2)}) %copy-start.1) | copy-done | bytes 16777240
  71.5 5.8 %copy-done.3 = bf16[8192,1024]{1,0:T(8,128)(2,1)S(1)} copy-done((bf16[8192,1024]{1,0:T(8,128)(2,1)S(1)}, bf16[8192,1024]{1,0:T(8,128)(2,1)}, u32[]{:S(2)}) %copy-start.3) | copy-done | bytes 16777240
  77.3 1.0 copy-done.8
  78.4 0.8 copy-done.10
  79.2 0.8 copy-done.12
  80.0 0.8 copy-done.14
  80.9 10.6 %shard_map.122 = (f32[2,8,8192]{2,1,0:T(8,128)S(1)}, bf16[2,8,8192]{2,1,0:T(8,128)(2,1)S(1)}, bf16[16,1024]{1,0:T(8,128)(2,1)S(1)}, bf16[32,64]{1,0:T(8,128)(2,1)S(1)}) custom-call(f32[16,8,64]{2,1,0:T(8,128)S(1)} %reshape.103.got_ref, f32[16,1]{1,0:T(8,128)S(1)} %slice_add_fusion.slot_ref, f32[16,1024]{1,0:T(8,128)S(1)} %copy-done.10, ...), custom_call_target="tpu_custom_call" | custom-call | tf_op jit(solution)/shard_map/pallas_call | solution.py:182
  91.5 0.3 collective-permute-start.1
  91.8 1.2 %collective-permute-done.1 = bf16[2,8,8192]{2,1,0:T(8,128)(2,1)S(1)} collective-permute-done((bf16[2,8,8192]{2,1,0:T(8,128)(2,1)S(1)}, bf16[2,8,8192]{2,1,0:T(8,128)(2,1)S(1)}, u32[]{:S(2)}, u32[]{:S(2)}) %collective-permute-start.1) | collective-permute-done | bytes 262176 | tf_op jit(solution)/shard_map/ppermute | solution.py:284
  93.1 0.1 fusion
  93.1 1.0 copy.27
  94.1 5.9 %all-to-all-start.2 = ((bf16[8,2,8192]{2,1,0:T(2,128)(2,1)}), bf16[8,2,8192]{2,1,0:T(2,128)(2,1)S(1)}, u32[]{:S(2)}, u32[]{:S(2)}) async-start(bf16[8,2,8192]{2,1,0:T(2,128)(2,1)} %copy.27), calls=%async_computation.2 | async-start | bytes 524288 | tf_op jit(solution)/shard_map/all_to_all | solution.py:288
  100.0 2.7 %shard_map.123 = (bf16[1024,1024]{1,0:T(8,128)(2,1)}, bf16[64,8192]{1,0:T(8,128)(2,1)}) custom-call(bf16[16,1024]{1,0:T(8,128)(2,1)S(1)} %get-tuple-element.24.left_ref, bf16[16,1024]{1,0:T(8,128)(2,1)S(1)} %get-tuple-element.19.hid_ref, bf16[32,64]{1,0:T(8,128)(2,1)S(1)} %get-tuple-element.25.weighted_ref, bf16[16,8192]{1,0:T(8,128)(2,1)S(1)} %get-tuple-element.28.c_ref), custom_call_target="tpu_custom_call" | custom-call | flops 33554432 | bytes 3145728 | tf_op jit(solution)/shard_map/pallas_call | solution.py:182
  102.7 6.5 %all-to-all-done.2 = bf16[8,2,8192]{2,1,0:T(2,128)(2,1)S(1)} async-done(((bf16[8,2,8192]{2,1,0:T(2,128)(2,1)}), bf16[8,2,8192]{2,1,0:T(2,128)(2,1)S(1)}, u32[]{:S(2)}, u32[]{:S(2)}) %all-to-all-start.2) | async-done | bytes 262176 | tf_op jit(solution)/shard_map/all_to_all | solution.py:288
  109.2 0.2 reduce_sum.22
  109.4 0.7 fusion.4
  (14 shorter events, 0.1 us)
Async XLA Ops:
  0.6 24.6 %copy-start.6 = (bf16[4,16,8192]{2,1,0:T(8,128)(2,1)S(1)}, bf16[4,16,8192]{2,1,0:T(8,128)(2,1)}, u32[]{:S(2)}) copy-start(bf16[4,16,8192]{2,1,0:T(8,128)(2,1)} %param.17) | copy-start | bytes 3145732
  0.6 24.6 %copy-start.5 = (bf16[64,16,1024]{2,1,0:T(8,128)(2,1)S(1)}, bf16[64,16,1024]{2,1,0:T(8,128)(2,1)}, u32[]{:S(2)}) copy-start(bf16[64,16,1024]{2,1,0:T(8,128)(2,1)} %param.16) | copy-start | bytes 6291460
  23.5 1.6 %collective-permute-start = (bf16[8,1,2,8320]{3,0,2,1:T(8,128)(2,1)S(1)}, bf16[8,1,2,8320]{3,0,2,1:T(8,128)(2,1)S(1)}, u32[]{:S(2)}, u32[]{:S(2)}) collective-permute-start(bf16[8,1,2,8320]{3,0,2,1:T(8,128)(2,1)S(1)} %copy.23), channel_id=1, source_target_pairs={{0,1},{1,0},{2,3},{3,2},{4,5},{5,4},{6,7},{7,6},{8,9},{9,8},{10,11... | collective-permute-start | bytes 798728 | tf_op jit(solution)/shard_map/ppermute | solution.py:244
  25.3 5.8 %copy-start = (bf16[8192,1024]{1,0:T(8,128)(2,1)S(1)}, bf16[8192,1024]{1,0:T(8,128)(2,1)}, u32[]{:S(2)}) copy-start(bf16[8192,1024]{1,0:T(8,128)(2,1)} %wg_ref.3) | copy-start | bytes 50331652
  31.1 5.8 %copy-start.2 = (bf16[8192,1024]{1,0:T(8,128)(2,1)S(1)}, bf16[8192,1024]{1,0:T(8,128)(2,1)}, u32[]{:S(2)}) copy-start(bf16[8192,1024]{1,0:T(8,128)(2,1)} %wu_ref.3) | copy-start | bytes 50331652
  43.0 0.7 copy-start.11
  43.6 19.4 %copy-start.9 = (f32[16,1024]{1,0:T(8,128)}, f32[16,1024]{1,0:T(8,128)S(1)}, u32[]{:S(2)}) copy-start(f32[16,1024]{1,0:T(8,128)S(1)} %get-tuple-element.17.gate_ref) | copy-start | bytes 196612
  45.8 18.6 %all-to-all-start.1 = ((f32[16,1,512]{2,1,0:T(1,128)}), f32[16,1,512]{2,1,0:T(1,128)S(1)}, u32[]{:S(2)}, u32[]{:S(2)}) async-start(f32[16,1,512]{2,1,0:T(1,128)} %reshape.102), calls=%async_computation.1 | async-start | bytes 65536 | tf_op jit(solution)/shard_map/all_to_all | solution.py:262
  49.3 5.8 %copy-start.4 = (bf16[1024,8192]{1,0:T(8,128)(2,1)S(1)}, bf16[1024,8192]{1,0:T(8,128)(2,1)}, u32[]{:S(2)}) copy-start(bf16[1024,8192]{1,0:T(8,128)(2,1)} %wd_ref.1) | copy-start | bytes 50331652
  63.0 0.8 copy-start.7
  63.8 0.6 copy-start.13
  65.8 5.8 %copy-start.1 = (bf16[8192,1024]{1,0:T(8,128)(2,1)S(1)}, bf16[8192,1024]{1,0:T(8,128)(2,1)}, u32[]{:S(2)}) copy-start(bf16[8192,1024]{1,0:T(8,128)(2,1)} %wg_ref.3) | copy-start | bytes 50331652
  71.5 5.8 %copy-start.3 = (bf16[8192,1024]{1,0:T(8,128)(2,1)S(1)}, bf16[8192,1024]{1,0:T(8,128)(2,1)}, u32[]{:S(2)}) copy-start(bf16[8192,1024]{1,0:T(8,128)(2,1)} %wu_ref.3) | copy-start | bytes 50331652
  77.3 1.0 copy-start.8
  78.3 0.8 copy-start.10
  79.2 0.8 copy-start.12
  80.0 0.8 copy-start.14
  91.5 1.6 %collective-permute-start.1 = (bf16[2,8,8192]{2,1,0:T(8,128)(2,1)S(1)}, bf16[2,8,8192]{2,1,0:T(8,128)(2,1)S(1)}, u32[]{:S(2)}, u32[]{:S(2)}) collective-permute-start(bf16[2,8,8192]{2,1,0:T(8,128)(2,1)S(1)} %get-tuple-element.23), channel_id=1, source_target_pairs={{0,1},{1,0},{2,3},{3,2},{4,5},{5,4},{6,7},{7,6},{8,9},{9,8},{10,11... | collective-permute-start | bytes 786440 | tf_op jit(solution)/shard_map/ppermute | solution.py:284
  94.1 15.1 %all-to-all-start.2 = ((bf16[8,2,8192]{2,1,0:T(2,128)(2,1)}), bf16[8,2,8192]{2,1,0:T(2,128)(2,1)S(1)}, u32[]{:S(2)}, u32[]{:S(2)}) async-start(bf16[8,2,8192]{2,1,0:T(2,128)(2,1)} %copy.27), calls=%async_computation.2 | async-start | bytes 524288 | tf_op jit(solution)/shard_map/all_to_all | solution.py:288

commit v2 on v1

v2 whole, which is shorter than its diff:
```python
import functools

import jax
import jax.numpy as jnp
from jax import lax
from jax.experimental import pallas as pl
from jax.experimental.pallas import tpu as pltpu
from jax.sharding import PartitionSpec as P

adapter_scale = 2.0
f32 = jnp.float32
bf16 = jnp.bfloat16
AHEAD = 5
PARTS = 2
PIECE = 1 << 20
SPLIT = 128
VMEM = pl.BlockSpec(memory_space=pltpu.VMEM)
SMEM = pl.BlockSpec(memory_space=pltpu.SMEM)
HBM = pl.BlockSpec(memory_space=pltpu.HBM)
NT = (((1,), (1,)), ((), ()))
TN = (((0,), (0,)), ((), ()))


def params(mib):
    return pltpu.CompilerParams(vmem_limit_bytes=mib << 20)


def fit(size, want):
    return want if size % want == 0 else size


def slot_mask(slot, first, columns, rank):
    col = lax.broadcasted_iota(jnp.int32, (slot.shape[0], columns), 1) // rank
    return slot.astype(jnp.int32) == col + first


def fold_matrix(columns, rank, by_row):
    shape = (columns, rank) if by_row else (rank, columns)
    c = lax.broadcasted_iota(jnp.int32, shape, 0 if by_row else 1)
    r = lax.broadcasted_iota(jnp.int32, shape, 1 if by_row else 0)
    return jnp.where(c % rank == r, 1.0, 0.0).astype(bf16)


def halves(v):
    high = v.astype(bf16)
    return high, (v - high.astype(f32)).astype(bf16)


def dot(a, b, dims=(((1,), (0,)), ((), ()))):
    return lax.dot_general(a, b, dims, preferred_element_type=f32)


def dot2(v, b, dims=(((1,), (0,)), ((), ()))):
    high, low = halves(v)
    return dot(high, b, dims) + dot(low, b, dims)


class Stream:
    def __init__(self, ahead):
        self.moves, self.ahead, self.taken, self.begun = [], ahead, 0, 0

    def add(self, src, dst, sem):
        self.moves.append(pltpu.make_async_copy(src, dst, sem))

    def fill(self):
        while self.begun < min(self.taken + self.ahead, len(self.moves)):
            self.moves[self.begun].start()
            self.begun += 1

    def take(self, count=1):
        for _ in range(count):
            self.fill()
            self.moves[self.taken].wait()
            self.taken += 1
        self.fill()


def pack_kernel(
    index_ref, table_hbm, tokens_hbm, cotangent_hbm, out_ref,
    table_ref, tokens_ref, cotangent_ref, sems,
):
    moves = [
        pltpu.make_async_copy(a, b, sems.at[i])
        for i, (a, b) in enumerate(
            (
                (table_hbm, table_ref),
                (tokens_hbm, tokens_ref),
                (cotangent_hbm, cotangent_ref),
            )
        )
    ]
    for m in moves:
        m.start()
    for m in moves:
        m.wait()
    width = tokens_ref.shape[1]
    slot = table_ref[index_ref[0]]
    lane = lax.broadcasted_iota(jnp.int32, (1, SPLIT), 1)
    digits = jnp.where(lane == 0, slot // SPLIT, jnp.where(lane == 1, slot % SPLIT, 0))
    digits = digits.astype(f32).astype(bf16)
    for i in range(out_ref.shape[0]):
        out_ref[i, 0:1, :width] = tokens_ref[...]
        out_ref[i, 1:2, :width] = cotangent_ref[...]
        out_ref[i, 0:1, width:] = digits
        out_ref[i, 1:2, width:] = digits


def blocks(size, step):
    return [pl.ds(i * step, step) for i in range(size // step)]


def forward_kernel(
    rank, parts,
    x_ref, c_ref, slot_ref, wg_hbm, wu_hbm, wd_hbm, d_hbm, u_hbm,
    gate_ref, up_ref, hid_ref, pay_ref, base_ref, pull_ref, wg_ref, d_ref, u_ref,
    wu_ref, wd_ref, sg, su, sd, sf,
):
    total, width = x_ref.shape
    hidden_dev = wg_ref.shape[1]
    units = hidden_dev // parts
    tall = fit(width, PIECE // units)
    flat = fit(units, PIECE // width)
    stream = Stream(AHEAD)
    stream.add(u_hbm, u_ref, sf.at[0])
    for p, f in enumerate(blocks(hidden_dev, units)):
        for j, k in enumerate(blocks(width, tall)):
            stream.add(wg_hbm.at[k, f], wg_ref.at[k, f], sg.at[p, j])
        for j, k in enumerate(blocks(width, tall)):
            stream.add(wu_hbm.at[k, f], wu_ref.at[k], su.at[p, j])
        if p == parts - 1:
            stream.add(d_hbm, d_ref, sf.at[1])
        for j, k in enumerate(blocks(units, flat)):
            at = pl.ds(p * units + j * flat, flat)
            stream.add(wd_hbm.at[at], wd_ref.at[k], sd.at[p, j])
    stream.fill()
    half = total // 2
    slot = slot_ref[...]

    stream.take()
    kept = u_ref.shape[0]
    first = lax.axis_index("tensor") * (kept // rank)
    pulled = dot(c_ref[...], u_ref[...], NT)
    pulled = jnp.where(slot_mask(slot, first, kept, rank), pulled, 0.0)
    rank_out = adapter_scale * dot2(pulled, fold_matrix(kept, rank, True))

    def project(w_ref, f):
        acc = jnp.zeros((total, units), f32)
        for k in blocks(width, tall):
            stream.take()
            acc = acc + dot(x_ref[:, k], w_ref[k, f])
        return acc

    step = fit(width, 2048)
    for p, f in enumerate(blocks(hidden_dev, units)):
        gate = project(wg_ref, f)
        gate_ref[:, f] = gate
        up = project(wu_ref, slice(None))
        up_ref[:, f] = up
        hid = (gate * jax.nn.sigmoid(gate) * up).astype(bf16)
        hid_ref[:, f] = hid
        if p == parts - 1:
            stream.take()
            columns = d_ref.shape[0]
            met = dot(hid_ref[...], d_ref[...], NT)
            met = jnp.where(slot_mask(slot, 0, columns, rank), met, 0.0)
            rank_in = dot2(met, fold_matrix(columns, rank, True))
        for j, k in enumerate(blocks(units, flat)):
            stream.take()
            at = pl.ds(p * units + j * flat, flat)
            pull_ref[:, at] = dot(c_ref[...], wd_ref[k], NT)
        for s in blocks(width, step):
            part = dot(hid, wd_ref[:, s])
            base_ref[:, s] = part if p == 0 else base_ref[:, s] + part

    both = jnp.concatenate((rank_in, rank_out), axis=1)
    swap = lax.axis_index("tensor") % 2
    own, sib = both[:half], both[half:]
    pay = jnp.concatenate(
        (
            jnp.where(swap == 0, own, sib),
            jnp.where(swap == 0, sib, own),
            jnp.zeros((half, pay_ref.shape[2] - 4 * rank), f32),
        ),
        axis=1,
    )
    for i in range(pay_ref.shape[0]):
        pay_ref[i] = pay


def backward_kernel(
    rank,
    got_ref, slot_ref, gate_ref, up_ref, base_ref, pull_ref, wg_ref, wu_hbm, d_ref, u_ref,
    own_ref, sib_ref, left_ref, weighted_ref,
    wu_ref, su,
):
    total, hidden_dev = gate_ref.shape
    width = wg_ref.shape[0]
    piece = fit(width, 1024)
    stream = Stream(AHEAD)
    for j, k in enumerate(blocks(width, piece)):
        stream.add(wu_hbm.at[k], wu_ref.at[k], su.at[j])
    stream.fill()
    half = total // 2
    columns = d_ref.shape[0]
    kept = u_ref.shape[0]
    got = jnp.sum(got_ref[...], axis=0)
    swap = lax.axis_index("tensor") % 2
    a, b = got[:, : 2 * rank], got[:, 2 * rank : 4 * rank]
    both = jnp.concatenate(
        (jnp.where(swap == 0, a, b), jnp.where(swap == 0, b, a)), axis=0
    )
    rank_in = both[:, :rank]
    rank_out = both[:, rank:].astype(bf16)
    spread = dot(rank_out, fold_matrix(columns, rank, False))
    slot = slot_ref[...]
    left = jnp.where(slot_mask(slot, 0, columns, rank), spread, 0.0).astype(bf16)
    left_ref[...] = left
    grad = pull_ref[...] + dot(left, d_ref[...])
    gate = gate_ref[...]
    up = up_ref[...]
    sig = jax.nn.sigmoid(gate)
    gg = (grad * up * sig * (1.0 + gate * (1.0 - sig))).astype(bf16)
    gu = (grad * (gate * sig)).astype(bf16)
    first = lax.axis_index("tensor") * (kept // rank)
    mine = slot_mask(slot, first, kept, rank)
    high, low = halves(rank_in)
    fold = fold_matrix(kept, rank, False)
    high = jnp.where(mine, dot(high, fold), 0.0).astype(bf16)
    low = jnp.where(mine, dot(low, fold), 0.0).astype(bf16)
    weighted_ref[...] = jnp.concatenate((high, low), axis=0)
    for s in blocks(width, 2 * piece):
        us = u_ref[:, s]
        adapted = adapter_scale * (dot(high, us) + dot(low, us))
        out = base_ref[:, s] + adapted.astype(bf16).astype(f32)
        own_ref[0, :, s] = out[:half]
        sib_ref[0, :, s] = out[half:].astype(bf16)
        inp = dot(gg, wg_ref[s, :], NT)
        stream.take(2)
        inp = inp + dot(gu, wu_ref[s, :], NT)
        own_ref[1, :, s] = inp[:half]
        sib_ref[1, :, s] = inp[half:].astype(bf16)


def factor_kernel(left_ref, hid_ref, weighted_ref, c_ref, down_ref, upg_ref):
    columns = down_ref.shape[0]
    rows = fit(columns, 256)
    for i in range(columns // rows):
        s = pl.ds(i * rows, rows)
        down_ref[s, :] = dot(left_ref[:, s], hid_ref[...], TN).astype(bf16)
    width = c_ref.shape[1]
    chunk = fit(width, 1024)
    total = c_ref.shape[0]
    for i in range(width // chunk):
        s = pl.ds(i * chunk, chunk)
        cs = c_ref[:, s]
        both = dot(weighted_ref[:total], cs, TN) + dot(weighted_ref[total:], cs, TN)
        upg_ref[:, s] = (adapter_scale * both).astype(bf16)


def call(kernel, args, outs, mib, specs=None, out_specs=None, flops=0, nbytes=0, scratch=()):
    return pl.pallas_call(
        kernel,
        in_specs=specs or [VMEM] * len(args),
        out_specs=out_specs or [VMEM] * len(outs),
        out_shape=[jax.ShapeDtypeStruct(*o) if isinstance(o, tuple) else o for o in outs],
        scratch_shapes=scratch,
        compiler_params=params(mib),
        cost_estimate=pl.CostEstimate(flops=flops, bytes_accessed=nbytes, transcendentals=0),
    )(*args)


def held(x):
    return pltpu.with_memory_space_constraint(x, pltpu.VMEM)


def far(x):
    return pltpu.with_memory_space_constraint(x, pltpu.HBM)


def per_device(
    tokens,
    cotangent,
    token_adapter_index,
    adapter_storage_slot,
    gate_weight,
    up_weight,
    down_weight,
    adapter_down_factors,
    adapter_up_factors,
):
    devices = lax.axis_size("tensor")
    chips = devices // 2
    tok_dev, width = tokens.shape
    hidden_dev = gate_weight.shape[1]
    kept, rank = adapter_up_factors.shape[:2]
    count = adapter_storage_slot.shape[0]
    half = chips * tok_dev
    total = 2 * half
    room = 4 if total <= 16 else 40
    same_core = [[c + 2 * i for i in range(chips)] for c in range(2)]
    pairs = [(i, i ^ 1) for i in range(devices)]
    parts = PARTS if hidden_dev % (256 * PARTS) == 0 else 1
    units = hidden_dev // parts

    wg, wu, wd = far(gate_weight), far(up_weight), far(down_weight)
    d = far(adapter_down_factors.reshape(count * rank, hidden_dev))
    u = far(adapter_up_factors.reshape(kept * rank, width))
    weight_mib = -(-2 * width * hidden_dev >> 20)

    (sent,) = call(
        pack_kernel,
        (token_adapter_index, far(adapter_storage_slot), far(tokens), far(cotangent)),
        (((chips, 2, width + SPLIT), bf16),),
        room,
        specs=[SMEM] + [HBM] * 3,
        scratch=[
            pltpu.SMEM(adapter_storage_slot.shape, jnp.int32),
            pltpu.VMEM(tokens.shape, bf16),
            pltpu.VMEM(cotangent.shape, bf16),
            pltpu.SemaphoreType.DMA((3,)),
        ],
    )
    own = lax.all_to_all(sent, "tensor", 0, 0, axis_index_groups=same_core, tiled=True)
    sib = lax.ppermute(own, "tensor", pairs)
    gathered = jnp.concatenate((own, sib), axis=0).reshape(total, 2, width + SPLIT)
    x = gathered[:, 0, :width]
    c = gathered[:, 1, :width]
    code = gathered[:, 0, width : width + 2].astype(f32)
    slots = code[:, 0:1] * SPLIT + code[:, 1:2]

    sems = pltpu.SemaphoreType.DMA
    gate, up, hid, pay, base, pull, wg, d, u = call(
        functools.partial(forward_kernel, rank, parts),
        (x, c, slots, wg, wu, wd, d, u),
        (
            ((total, hidden_dev), f32),
            ((total, hidden_dev), f32),
            ((total, hidden_dev), bf16),
            ((devices, half, -(-4 * rank // 128) * 128), f32),
            ((total, width), f32),
            ((total, hidden_dev), f32),
            pltpu.VMEM(wg.shape, bf16),
            pltpu.VMEM(d.shape, bf16),
            pltpu.VMEM(u.shape, bf16),
        ),
        room + -(-2 * weight_mib // parts),
        specs=[VMEM] * 3 + [HBM] * 5,
        scratch=[
            pltpu.VMEM((width, units), bf16),
            pltpu.VMEM((units, width), bf16),
            sems((parts, width // fit(width, PIECE // units))),
            sems((parts, width // fit(width, PIECE // units))),
            sems((parts, units // fit(units, PIECE // width))),
            sems((2,)),
        ],
    )
    got = lax.all_to_all(pay, "tensor", 0, 0)
    mine, theirs, left, weighted = call(
        functools.partial(backward_kernel, rank),
        (got, slots, gate, up, base, pull, held(wg), wu, held(d), held(u)),
        (
            ((2, half, width), f32),
            ((2, half, width), bf16),
            ((total, count * rank), bf16),
            ((2 * total, kept * rank), bf16),
        ),
        room + 6 + weight_mib,
        specs=[VMEM] * 7 + [HBM, VMEM, VMEM],
        scratch=[pltpu.VMEM(wu.shape, bf16), sems((width // fit(width, 1024),))],
    )
    summed = mine + lax.ppermute(theirs, "tensor", pairs).astype(f32)
    summed = jnp.transpose(
        summed.astype(bf16).reshape(2, chips, tok_dev, width), (1, 0, 2, 3)
    ).reshape(chips, 2 * tok_dev, width)
    back = lax.all_to_all(summed, "tensor", 0, 0, axis_index_groups=same_core, tiled=True)
    down_grad, up_factor_gradient = call(
        factor_kernel,
        (left, hid, weighted, c),
        (((count * rank, hidden_dev), bf16), ((kept * rank, width), bf16)),
        room,
        flops=2 * total * count * rank * hidden_dev,
        nbytes=2 * (count * rank * hidden_dev + kept * rank * width),
    )
    final = jnp.sum(back.astype(f32).reshape(chips, 2, tok_dev, width), axis=0).astype(bf16)
    return (
        final[0],
        final[1],
        down_grad.reshape(count, rank, hidden_dev),
        up_factor_gradient.reshape(kept, rank, width),
    )


def solution(mesh):
    in_specs = (
        P(("parts", "tensor"), None),
        P(("parts", "tensor"), None),
        P(("parts", "tensor")),
        P(),
        P(None, "tensor"),
        P(None, "tensor"),
        P("tensor", None),
        P(None, None, "tensor"),
        P("tensor", None, None),
    )
    out_specs = (
        P(("parts", "tensor"), None),
        P(("parts", "tensor"), None),
        P("parts", None, "tensor"),
        P(("parts", "tensor"), None, None),
    )
    return jax.shard_map(
        per_device, mesh=mesh, in_specs=in_specs, out_specs=out_specs, check_vma=False
    )
```

time: 111 us -> 84.2 us (0.76)
  local copies, waits for them, and re-layouts: 39.1 us -> 1.74 us
  Pallas kernels: 27.4 us -> 40.6 us
  blocking collectives: 16.9 us -> 26.5 us
  starting transfers between devices: 9.75 us -> 3.55 us
  other arithmetic: 3.51 us -> 0.37 us
  between operations: 4.18 us -> 1.35 us
    unnamed x32 -> x0, local copies, waits for them, and re-layouts: 36.1 us -> none
    pallas_call x4, Pallas kernels: 27.4 us -> 40.6 us  [call(): pl.pallas_call(kernel, in_specs=specs or [VMEM] * len(args), out_specs=ou...]
    all_to_all x0 -> x1, blocking collectives: none -> 9.64 us  [per_device(): got = lax.all_to_all(pay, 'tensor', 0, 0)]
    all_to_all x1 -> x0, starting transfers between devices: 3.5 us -> none  [per_device(): lax.all_to_all(jnp.broadcast_to(pay[None], (devices,) + pay.shape), 'tens...]
    all_to_all x1, starting transfers between devices: 5.87 us -> 3.41 us  [per_device(): lax.all_to_all(summed, 'tensor', 0, 0, axis_index_groups=same_core, tiled...]
    reduce_sum x1 -> x0, other arithmetic: 1.44 us -> none  [per_device(): jnp.sum(jnp.where(token_adapter_index[:, None] == table[None, :], adapter...]
  transfers between devices with their start and end apart: 4 -> 3, of which waited for: 3 -> 3; matrix products, arithmetic and copies ran while one was open for 0% -> 0% of each run, Pallas kernels for 10% -> 3%
where the time goes in v2:
time: 84.2 us; the launch traced here: 83.8 us
  Pallas kernels  40.6 us (48%)
  blocking collectives  26.5 us (31%)
  waiting for transfers between devices  9.76 us (12%)
  starting transfers between devices  3.55 us (4%)
  local copies, waits for them, and re-layouts  1.74 us (2%)
  between operations  1.35 us (2%)
    pallas_call x4, Pallas kernels, call(): pl.pallas_call(kernel, in_specs=specs or [VMEM] * len(args), out_specs=ou...  40.6 us
    all_to_all x1, blocking collectives, per_device(): lax.all_to_all(sent, 'tensor', 0, 0, axis_index_groups=same_core, tiled=T...  16.9 us
    all_to_all x1, blocking collectives, per_device(): got = lax.all_to_all(pay, 'tensor', 0, 0)  9.64 us
    all_to_all x1, waiting for transfers between devices, per_device(): lax.all_to_all(summed, 'tensor', 0, 0, axis_index_groups=same_core, tiled...  6.71 us
    all_to_all x1, starting transfers between devices, per_device(): lax.all_to_all(summed, 'tensor', 0, 0, axis_index_groups=same_core, tiled...  3.41 us
  transfers between devices with their start and end apart: 3, of which 3 were waited for; matrix products, arithmetic and copies ran while one was open for 0% of the time, Pallas kernels for 3%

profile of v2, /device:TPU:0, one launch (start us, length us, event | category | flops | bytes accessed | tf_op | source)
XLA Modules:
  0.0 83.8 jit_solution(8243299322023619441)
XLA Ops:
  1.3 0.9 %shard_map.120 = bf16[8,2,8320]{2,1,0:T(2,128)(2,1)S(1)} custom-call(s32[1]{0:T(128)S(6)} %copy.33.index_ref, s32[64]{0:T(128)} %table_hbm.1, bf16[1,8192]{1,0:T(2,128)(2,1)} %tokens_hbm.1, bf16[1,8192]{1,0:T(2,128)(2,1)} %cotangent_hbm.1), custom_call_target="tpu_custom_call" | custom-call | tf_op jit(solution)/shard_map/pallas_call | solution.py:261
  2.1 16.9 %all_to_all.15 = bf16[8,2,8320]{2,1,0:T(2,128)(2,1)S(1)} all-to-all(bf16[8,2,8320]{2,1,0:T(2,128)(2,1)S(1)} %shard_map.120), channel_id=1, replica_groups={{0,2,4,6,8,10,12,14},{1,3,5,7,9,11,13,15},{16,18,20,22,24,26,28,30},{17..., dimensions={0} | all-to-all | bytes 532480 | tf_op jit(solution)/shard_map/all_to_all | solution.py:323
  19.0 0.1 collective-permute-start
  19.1 1.5 %collective-permute-done = bf16[8,2,8320]{2,0,1:T(8,128)(2,1)S(1)} collective-permute-done((bf16[8,2,8320]{2,0,1:T(8,128)(2,1)S(1)}, bf16[8,2,8320]{2,0,1:T(8,128)(2,1)S(1)}, u32[]{:S(2)}, u32[]{:S(2)}) %collective-permute-start) | collective-permute-done | bytes 266272 | tf_op jit(solution)/shard_map/ppermute | solution.py:324
  20.7 0.1 slice_add_fusion.slot_ref
  20.8 23.8 %shard_map.121 = (f32[16,1024]{1,0:T(8,128)S(1)}, f32[16,1024]{1,0:T(8,128)S(1)}, bf16[16,1024]{1,0:T(8,128)(2,1)S(1)}, f32[16,8,128]{2,1,0:T(8,128)S(1)}, f32[1...) custom-call(bf16[16,8192]{1,0:T(8,128)(2,1)S(1)} %get-tuple-element., ...), custom_call_target="tpu_custom_call" | custom-call | tf_op jit(solution)/shard_map/pallas_call | solution.py:261
  44.6 9.6 %all_to_all.16.got_ref = f32[16,8,128]{2,1,0:T(8,128)S(1)} all-to-all(f32[16,8,128]{2,1,0:T(8,128)S(1)} %get-tuple-element.19), channel_id=1, replica_groups=mesh['parts'=2,'tensor'=16] {'tensor'}, dimensions={0} | all-to-all | bytes 131072 | tf_op jit(solution)/shard_map/all_to_all | solution.py:357
  54.2 13.2 %shard_map.122 = (f32[2,8,8192]{2,1,0:T(8,128)S(1)}, bf16[2,8,8192]{2,1,0:T(8,128)(2,1)S(1)}, bf16[16,1024]{1,0:T(8,128)(2,1)S(1)}, bf16[32,64]{1,0:T(8,128)(2,1)S(1)}) custom-call(f32[16,8,128]{2,1,0:T(8,128)S(1)} %all_to_all.16.got_ref, f32[16,1]{1,0:T(8,128)S(1)} %slice_add_fusion.slot_ref, f32[16,1024]{1,0:T(8,128)S(1)} %get-tuple-element.20.gate_ref, ...), custom_call_target="tpu_custom_call" | custom-call | tf_op jit(solution)/shard_map/pallas_call | solution.py:261
  67.4 0.1 collective-permute-start.1
  67.5 1.5 %collective-permute-done.1 = bf16[2,8,8192]{2,1,0:T(8,128)(2,1)S(1)} collective-permute-done((bf16[2,8,8192]{2,1,0:T(8,128)(2,1)S(1)}, bf16[2,8,8192]{2,1,0:T(8,128)(2,1)S(1)}, u32[]{:S(2)}, u32[]{:S(2)}) %collective-permute-start.1) | collective-permute-done | bytes 262176 | tf_op jit(solution)/shard_map/ppermute | solution.py:371
  69.1 1.0 %copy.28 = bf16[8,2,8192]{2,1,0:T(2,128)(2,1)} copy(bf16[8,2,8192]{2,0,1:T(8,128)(2,1)S(1)} %fusion) | data formatting | bytes 524288 | tf_op jit(solution)/shard_map/reshape | solution.py:374
  70.1 3.4 %all-to-all-start.2 = ((bf16[8,2,8192]{2,1,0:T(2,128)(2,1)}), bf16[8,2,8192]{2,1,0:T(2,128)(2,1)S(1)}, u32[]{:S(2)}, u32[]{:S(2)}) async-start(bf16[8,2,8192]{2,1,0:T(2,128)(2,1)} %copy.28), calls=%async_computation.2 | async-start | bytes 524288 | tf_op jit(solution)/shard_map/all_to_all | solution.py:375
  73.5 2.7 %shard_map.123 = (bf16[1024,1024]{1,0:T(8,128)(2,1)}, bf16[64,8192]{1,0:T(8,128)(2,1)}) custom-call(bf16[16,1024]{1,0:T(8,128)(2,1)S(1)} %get-tuple-element.29.left_ref, bf16[16,1024]{1,0:T(8,128)(2,1)S(1)} %get-tuple-element.30.hid_ref, bf16[32,64]{1,0:T(8,128)(2,1)S(1)} %get-tuple-element.31.weighted_ref, bf16[16,8192]{1,0:T(8,128)(2,1)S(1)} %get-tuple-element.34.c_ref), custom_call_target="tpu_custom_call" | custom-call | flops 33554432 | bytes 3145728 | tf_op jit(solution)/shard_map/pallas_call | solution.py:261
  76.2 6.7 %all-to-all-done.2 = bf16[8,2,8192]{2,1,0:T(2,128)(2,1)S(1)} async-done(((bf16[8,2,8192]{2,1,0:T(2,128)(2,1)}), bf16[8,2,8192]{2,1,0:T(2,128)(2,1)S(1)}, u32[]{:S(2)}, u32[]{:S(2)}) %all-to-all-start.2) | async-done | bytes 262176 | tf_op jit(solution)/shard_map/all_to_all | solution.py:375
  82.9 0.2 reduce_sum.12
  83.2 0.7 fusion.3
  (5 shorter events, 0.2 us)
Async XLA Ops:
  19.0 1.6 %collective-permute-start = (bf16[8,2,8320]{2,0,1:T(8,128)(2,1)S(1)}, bf16[8,2,8320]{2,0,1:T(8,128)(2,1)S(1)}, u32[]{:S(2)}, u32[]{:S(2)}) collective-permute-start(bf16[8,2,8320]{2,0,1:T(8,128)(2,1)S(1)} %get-tuple-element.36), channel_id=1, source_target_pairs={{0,1},{1,0},{2,3},{3,2},{4,5},{5,4},{6,7},{7,6},{8,9},{9,8},{10,11... | collective-permute-start | bytes 798728 | tf_op jit(solution)/shard_map/ppermute | solution.py:324
  67.4 1.6 %collective-permute-start.1 = (bf16[2,8,8192]{2,1,0:T(8,128)(2,1)S(1)}, bf16[2,8,8192]{2,1,0:T(8,128)(2,1)S(1)}, u32[]{:S(2)}, u32[]{:S(2)}) collective-permute-start(bf16[2,8,8192]{2,1,0:T(8,128)(2,1)S(1)} %get-tuple-element.28), channel_id=1, source_target_pairs={{0,1},{1,0},{2,3},{3,2},{4,5},{5,4},{6,7},{7,6},{8,9},{9,8},{10,11... | collective-permute-start | bytes 786440 | tf_op jit(solution)/shard_map/ppermute | solution.py:371
  70.1 12.9 %all-to-all-start.2 = ((bf16[8,2,8192]{2,1,0:T(2,128)(2,1)}), bf16[8,2,8192]{2,1,0:T(2,128)(2,1)S(1)}, u32[]{:S(2)}, u32[]{:S(2)}) async-start(bf16[8,2,8192]{2,1,0:T(2,128)(2,1)} %copy.28), calls=%async_computation.2 | async-start | bytes 524288 | tf_op jit(solution)/shard_map/all_to_all | solution.py:375

commit v3 on v2

--- a/solution.py
+++ b/solution.py
@@ -10,7 +10,7 @@
 adapter_scale = 2.0
 f32 = jnp.float32
 bf16 = jnp.bfloat16
-AHEAD = 5
+AHEAD = 8
 PARTS = 2
 PIECE = 1 << 20
 SPLIT = 128
@@ -145,8 +145,8 @@
 
     def project(w_ref, f):
         acc = jnp.zeros((total, units), f32)
-        for k in blocks(width, tall):
-            stream.take()
+        for k in blocks(width, fit(width, 2 * tall)):
+            stream.take(k.size // tall)
             acc = acc + dot(x_ref[:, k], w_ref[k, f])
         return acc
 
@@ -164,10 +164,8 @@
             met = dot(hid_ref[...], d_ref[...], NT)
             met = jnp.where(slot_mask(slot, 0, columns, rank), met, 0.0)
             rank_in = dot2(met, fold_matrix(columns, rank, True))
-        for j, k in enumerate(blocks(units, flat)):
-            stream.take()
-            at = pl.ds(p * units + j * flat, flat)
-            pull_ref[:, at] = dot(c_ref[...], wd_ref[k], NT)
+        stream.take(units // flat)
+        pull_ref[:, f] = dot(c_ref[...], wd_ref[...], NT)
         for s in blocks(width, step):
             part = dot(hid, wd_ref[:, s])
             base_ref[:, s] = part if p == 0 else base_ref[:, s] + part
@@ -234,11 +232,12 @@
         out = base_ref[:, s] + adapted.astype(bf16).astype(f32)
         own_ref[0, :, s] = out[:half]
         sib_ref[0, :, s] = out[half:].astype(bf16)
-        inp = dot(gg, wg_ref[s, :], NT)
         stream.take(2)
-        inp = inp + dot(gu, wu_ref[s, :], NT)
-        own_ref[1, :, s] = inp[:half]
-        sib_ref[1, :, s] = inp[half:].astype(bf16)
+        for i in range(8):
+            t = pl.ds(s.start + i * piece // 4, piece // 4)
+            inp = dot(gg, wg_ref[t, :], NT) + dot(gu, wu_ref[t, :], NT)
+            own_ref[1, :, t] = inp[:half]
+            sib_ref[1, :, t] = inp[half:].astype(bf16)
 
 
 def factor_kernel(left_ref, hid_ref, weighted_ref, c_ref, down_ref, upg_ref):
@@ -343,7 +342,7 @@
             pltpu.VMEM(d.shape, bf16),
             pltpu.VMEM(u.shape, bf16),
         ),
-        room + -(-2 * weight_mib // parts),
+        room + 6 + -(-2 * weight_mib // parts),
         specs=[VMEM] * 3 + [HBM] * 5,
         scratch=[
             pltpu.VMEM((width, units), bf16),

time: 84.2 us -> 79.8 us (0.948)
  Pallas kernels: 40.6 us -> 36.1 us
    pallas_call x4, Pallas kernels: 40.6 us -> 36.1 us  [call(): pl.pallas_call(kernel, in_specs=specs or [VMEM] * len(args), out_specs=ou...]
where the time goes in v3:
time: 79.8 us; the launch traced here: 79.4 us
  Pallas kernels  36.1 us (45%)
  blocking collectives  26.5 us (33%)
  waiting for transfers between devices  9.76 us (12%)
  starting transfers between devices  3.55 us (4%)
  local copies, waits for them, and re-layouts  1.74 us (2%)
  between operations  1.35 us (2%)
    pallas_call x4, Pallas kernels, call(): pl.pallas_call(kernel, in_specs=specs or [VMEM] * len(args), out_specs=ou...  36.1 us
    all_to_all x1, blocking collectives, per_device(): lax.all_to_all(sent, 'tensor', 0, 0, axis_index_groups=same_core, tiled=T...  16.9 us
    all_to_all x1, blocking collectives, per_device(): got = lax.all_to_all(pay, 'tensor', 0, 0)  9.64 us
    all_to_all x1, waiting for transfers between devices, per_device(): lax.all_to_all(summed, 'tensor', 0, 0, axis_index_groups=same_core, tiled...  6.71 us
    all_to_all x1, starting transfers between devices, per_device(): lax.all_to_all(summed, 'tensor', 0, 0, axis_index_groups=same_core, tiled...  3.41 us
  transfers between devices with their start and end apart: 3, of which 3 were waited for; matrix products, arithmetic and copies ran while one was open for 0% of the time, Pallas kernels for 3%

profile of v3, /device:TPU:0, one launch (start us, length us, event | category | flops | bytes accessed | tf_op | source)
XLA Modules:
  0.0 79.4 jit_solution(11249349192815023951)
XLA Ops:
  1.3 0.9 %shard_map.120 = bf16[8,2,8320]{2,1,0:T(2,128)(2,1)S(1)} custom-call(s32[1]{0:T(128)S(6)} %copy.33.index_ref, s32[64]{0:T(128)} %table_hbm.1, bf16[1,8192]{1,0:T(2,128)(2,1)} %tokens_hbm.1, bf16[1,8192]{1,0:T(2,128)(2,1)} %cotangent_hbm.1), custom_call_target="tpu_custom_call" | custom-call | tf_op jit(solution)/shard_map/pallas_call | solution.py:260
  2.1 16.9 %all_to_all.15 = bf16[8,2,8320]{2,1,0:T(2,128)(2,1)S(1)} all-to-all(bf16[8,2,8320]{2,1,0:T(2,128)(2,1)S(1)} %shard_map.120), channel_id=1, replica_groups={{0,2,4,6,8,10,12,14},{1,3,5,7,9,11,13,15},{16,18,20,22,24,26,28,30},{17..., dimensions={0} | all-to-all | bytes 532480 | tf_op jit(solution)/shard_map/all_to_all | solution.py:322
  19.0 0.1 collective-permute-start
  19.1 1.5 %collective-permute-done = bf16[8,2,8320]{2,0,1:T(8,128)(2,1)S(1)} collective-permute-done((bf16[8,2,8320]{2,0,1:T(8,128)(2,1)S(1)}, bf16[8,2,8320]{2,0,1:T(8,128)(2,1)S(1)}, u32[]{:S(2)}, u32[]{:S(2)}) %collective-permute-start) | collective-permute-done | bytes 266272 | tf_op jit(solution)/shard_map/ppermute | solution.py:323
  20.7 0.1 slice_add_fusion.slot_ref
  20.8 20.6 %shard_map.121 = (f32[16,1024]{1,0:T(8,128)S(1)}, f32[16,1024]{1,0:T(8,128)S(1)}, bf16[16,1024]{1,0:T(8,128)(2,1)S(1)}, f32[16,8,128]{2,1,0:T(8,128)S(1)}, f32[1...) custom-call(bf16[16,8192]{1,0:T(8,128)(2,1)S(1)} %get-tuple-element., ...), custom_call_target="tpu_custom_call" | custom-call | tf_op jit(solution)/shard_map/pallas_call | solution.py:260
  41.4 9.6 %all_to_all.16.got_ref = f32[16,8,128]{2,1,0:T(8,128)S(1)} all-to-all(f32[16,8,128]{2,1,0:T(8,128)S(1)} %get-tuple-element.19), channel_id=1, replica_groups=mesh['parts'=2,'tensor'=16] {'tensor'}, dimensions={0} | all-to-all | bytes 131072 | tf_op jit(solution)/shard_map/all_to_all | solution.py:356
  51.1 11.9 %shard_map.122 = (f32[2,8,8192]{2,1,0:T(8,128)S(1)}, bf16[2,8,8192]{2,1,0:T(8,128)(2,1)S(1)}, bf16[16,1024]{1,0:T(8,128)(2,1)S(1)}, bf16[32,64]{1,0:T(8,128)(2,1)S(1)}) custom-call(f32[16,8,128]{2,1,0:T(8,128)S(1)} %all_to_all.16.got_ref, f32[16,1]{1,0:T(8,128)S(1)} %slice_add_fusion.slot_ref, f32[16,1024]{1,0:T(8,128)S(1)} %get-tuple-element.20.gate_ref, ...), custom_call_target="tpu_custom_call" | custom-call | tf_op jit(solution)/shard_map/pallas_call | solution.py:260
  63.0 0.1 collective-permute-start.1
  63.1 1.5 %collective-permute-done.1 = bf16[2,8,8192]{2,1,0:T(8,128)(2,1)S(1)} collective-permute-done((bf16[2,8,8192]{2,1,0:T(8,128)(2,1)S(1)}, bf16[2,8,8192]{2,1,0:T(8,128)(2,1)S(1)}, u32[]{:S(2)}, u32[]{:S(2)}) %collective-permute-start.1) | collective-permute-done | bytes 262176 | tf_op jit(solution)/shard_map/ppermute | solution.py:370
  64.6 1.0 %copy.28 = bf16[8,2,8192]{2,1,0:T(2,128)(2,1)} copy(bf16[8,2,8192]{2,0,1:T(8,128)(2,1)S(1)} %fusion) | data formatting | bytes 524288 | tf_op jit(solution)/shard_map/reshape | solution.py:373
  65.6 3.4 %all-to-all-start.2 = ((bf16[8,2,8192]{2,1,0:T(2,128)(2,1)}), bf16[8,2,8192]{2,1,0:T(2,128)(2,1)S(1)}, u32[]{:S(2)}, u32[]{:S(2)}) async-start(bf16[8,2,8192]{2,1,0:T(2,128)(2,1)} %copy.28), calls=%async_computation.2 | async-start | bytes 524288 | tf_op jit(solution)/shard_map/all_to_all | solution.py:374
  69.0 2.7 %shard_map.123 = (bf16[1024,1024]{1,0:T(8,128)(2,1)}, bf16[64,8192]{1,0:T(8,128)(2,1)}) custom-call(bf16[16,1024]{1,0:T(8,128)(2,1)S(1)} %get-tuple-element.29.left_ref, bf16[16,1024]{1,0:T(8,128)(2,1)S(1)} %get-tuple-element.30.hid_ref, bf16[32,64]{1,0:T(8,128)(2,1)S(1)} %get-tuple-element.31.weighted_ref, bf16[16,8192]{1,0:T(8,128)(2,1)S(1)} %get-tuple-element.34.c_ref), custom_call_target="tpu_custom_call" | custom-call | flops 33554432 | bytes 3145728 | tf_op jit(solution)/shard_map/pallas_call | solution.py:260
  71.7 6.7 %all-to-all-done.2 = bf16[8,2,8192]{2,1,0:T(2,128)(2,1)S(1)} async-done(((bf16[8,2,8192]{2,1,0:T(2,128)(2,1)}), bf16[8,2,8192]{2,1,0:T(2,128)(2,1)S(1)}, u32[]{:S(2)}, u32[]{:S(2)}) %all-to-all-start.2) | async-done | bytes 262176 | tf_op jit(solution)/shard_map/all_to_all | solution.py:374
  78.4 0.2 reduce_sum.12
  78.7 0.7 fusion.3
  (5 shorter events, 0.2 us)
Async XLA Ops:
  19.0 1.6 %collective-permute-start = (bf16[8,2,8320]{2,0,1:T(8,128)(2,1)S(1)}, bf16[8,2,8320]{2,0,1:T(8,128)(2,1)S(1)}, u32[]{:S(2)}, u32[]{:S(2)}) collective-permute-start(bf16[8,2,8320]{2,0,1:T(8,128)(2,1)S(1)} %get-tuple-element.36), channel_id=1, source_target_pairs={{0,1},{1,0},{2,3},{3,2},{4,5},{5,4},{6,7},{7,6},{8,9},{9,8},{10,11... | collective-permute-start | bytes 798728 | tf_op jit(solution)/shard_map/ppermute | solution.py:323
  63.0 1.6 %collective-permute-start.1 = (bf16[2,8,8192]{2,1,0:T(8,128)(2,1)S(1)}, bf16[2,8,8192]{2,1,0:T(8,128)(2,1)S(1)}, u32[]{:S(2)}, u32[]{:S(2)}) collective-permute-start(bf16[2,8,8192]{2,1,0:T(8,128)(2,1)S(1)} %get-tuple-element.28), channel_id=1, source_target_pairs={{0,1},{1,0},{2,3},{3,2},{4,5},{5,4},{6,7},{7,6},{8,9},{9,8},{10,11... | collective-permute-start | bytes 786440 | tf_op jit(solution)/shard_map/ppermute | solution.py:370
  65.6 12.9 %all-to-all-start.2 = ((bf16[8,2,8192]{2,1,0:T(2,128)(2,1)}), bf16[8,2,8192]{2,1,0:T(2,128)(2,1)S(1)}, u32[]{:S(2)}, u32[]{:S(2)}) async-start(bf16[8,2,8192]{2,1,0:T(2,128)(2,1)} %copy.28), calls=%async_computation.2 | async-start | bytes 524288 | tf_op jit(solution)/shard_map/all_to_all | solution.py:374

commit v4 on v3

--- a/solution.py
+++ b/solution.py
@@ -256,6 +256,19 @@
         upg_ref[:, s] = (adapter_scale * both).astype(bf16)
 
 
+def combine_kernel(own_ref, got_ref, out_ref):
+    for i in range(own_ref.shape[0]):
+        both = own_ref[i] + got_ref[i].astype(f32)
+        out_ref[:, i, :] = both.astype(bf16)
+
+
+def finish_kernel(back_ref, mixed_ref, grad_ref):
+    total = jnp.sum(back_ref[...].astype(f32), axis=0).astype(bf16)
+    rows = mixed_ref.shape[0]
+    mixed_ref[...] = total[:rows]
+    grad_ref[...] = total[rows:]
+
+
 def call(kernel, args, outs, mib, specs=None, out_specs=None, flops=0, nbytes=0, scratch=()):
     return pl.pallas_call(
         kernel,
@@ -367,10 +380,12 @@
         specs=[VMEM] * 7 + [HBM, VMEM, VMEM],
         scratch=[pltpu.VMEM(wu.shape, bf16), sems((width // fit(width, 1024),))],
     )
-    summed = mine + lax.ppermute(theirs, "tensor", pairs).astype(f32)
-    summed = jnp.transpose(
-        summed.astype(bf16).reshape(2, chips, tok_dev, width), (1, 0, 2, 3)
-    ).reshape(chips, 2 * tok_dev, width)
+    (summed,) = call(
+        combine_kernel,
+        (mine, lax.ppermute(theirs, "tensor", pairs)),
+        (((half, 2, width), bf16),),
+        room,
+    )
     back = lax.all_to_all(summed, "tensor", 0, 0, axis_index_groups=same_core, tiled=True)
     down_grad, up_factor_gradient = call(
         factor_kernel,
@@ -380,10 +395,15 @@
         flops=2 * total * count * rank * hidden_dev,
         nbytes=2 * (count * rank * hidden_dev + kept * rank * width),
     )
-    final = jnp.sum(back.astype(f32).reshape(chips, 2, tok_dev, width), axis=0).astype(bf16)
+    mixed, input_grad = call(
+        finish_kernel,
+        (back,),
+        (((tok_dev, width), bf16), ((tok_dev, width), bf16)),
+        room,
+    )
     return (
-        final[0],
-        final[1],
+        mixed,
+        input_grad,
         down_grad.reshape(count, rank, hidden_dev),
         up_factor_gradient.reshape(kept, rank, width),
     )

time: 79.8 us -> 79.5 us (level)
  Pallas kernels: 36.1 us -> 37.8 us
  local copies, waits for them, and re-layouts: 1.74 us -> 0.1 us
    pallas_call x4 -> x6, Pallas kernels: 36.1 us -> 37.8 us  [call(): pl.pallas_call(kernel, in_specs=specs or [VMEM] * len(args), out_specs=ou...]
    reshape x1 -> x0, local copies, waits for them, and re-layouts: 0.97 us -> none  [per_device(): summed = jnp.transpose(summed.astype(bf16).reshape(2, chips, tok_dev, wid...]
where the time goes in v4:
time: 79.5 us; the launch traced here: 79.2 us
  Pallas kernels  37.8 us (48%)
  blocking collectives  26.5 us (33%)
  waiting for transfers between devices  9.76 us (12%)
  starting transfers between devices  3.55 us (4%)
  between operations  1.35 us (2%)
    pallas_call x6, Pallas kernels, call(): pl.pallas_call(kernel, in_specs=specs or [VMEM] * len(args), out_specs=ou...  37.8 us
    all_to_all x1, blocking collectives, per_device(): lax.all_to_all(sent, 'tensor', 0, 0, axis_index_groups=same_core, tiled=T...  16.9 us
    all_to_all x1, blocking collectives, per_device(): got = lax.all_to_all(pay, 'tensor', 0, 0)  9.64 us
    all_to_all x1, waiting for transfers between devices, per_device(): lax.all_to_all(summed, 'tensor', 0, 0, axis_index_groups=same_core, tiled...  6.71 us
    all_to_all x1, starting transfers between devices, per_device(): lax.all_to_all(summed, 'tensor', 0, 0, axis_index_groups=same_core, tiled...  3.41 us
  transfers between devices with their start and end apart: 3, of which 3 were waited for; matrix products, arithmetic and copies ran while one was open for 0% of the time, Pallas kernels for 3%

profile of v4, /device:TPU:0, one launch (start us, length us, event | category | flops | bytes accessed | tf_op | source)
XLA Modules:
  0.0 79.2 jit_solution(9795205740490120953)
XLA Ops:
  1.3 0.9 %shard_map.120 = bf16[8,2,8320]{2,1,0:T(2,128)(2,1)S(1)} custom-call(s32[1]{0:T(128)S(6)} %copy.31.index_ref, s32[64]{0:T(128)} %table_hbm.1, bf16[1,8192]{1,0:T(2,128)(2,1)} %tokens_hbm.1, bf16[1,8192]{1,0:T(2,128)(2,1)} %cotangent_hbm.1), custom_call_target="tpu_custom_call" | custom-call | tf_op jit(solution)/shard_map/pallas_call | solution.py:273
  2.1 16.9 %all_to_all.15 = bf16[8,2,8320]{2,1,0:T(2,128)(2,1)S(1)} all-to-all(bf16[8,2,8320]{2,1,0:T(2,128)(2,1)S(1)} %shard_map.120), channel_id=1, replica_groups={{0,2,4,6,8,10,12,14},{1,3,5,7,9,11,13,15},{16,18,20,22,24,26,28,30},{17..., dimensions={0} | all-to-all | bytes 532480 | tf_op jit(solution)/shard_map/all_to_all | solution.py:335
  19.0 0.1 collective-permute-start
  19.1 1.5 %collective-permute-done = bf16[8,2,8320]{2,0,1:T(8,128)(2,1)S(1)} collective-permute-done((bf16[8,2,8320]{2,0,1:T(8,128)(2,1)S(1)}, bf16[8,2,8320]{2,0,1:T(8,128)(2,1)S(1)}, u32[]{:S(2)}, u32[]{:S(2)}) %collective-permute-start) | collective-permute-done | bytes 266272 | tf_op jit(solution)/shard_map/ppermute | solution.py:336
  20.7 0.1 slice_add_fusion.slot_ref
  20.8 20.6 %shard_map.121 = (f32[16,1024]{1,0:T(8,128)S(1)}, f32[16,1024]{1,0:T(8,128)S(1)}, bf16[16,1024]{1,0:T(8,128)(2,1)S(1)}, f32[16,8,128]{2,1,0:T(8,128)S(1)}, f32[1...) custom-call(bf16[16,8192]{1,0:T(8,128)(2,1)S(1)} %get-tuple-element., ...), custom_call_target="tpu_custom_call" | custom-call | tf_op jit(solution)/shard_map/pallas_call | solution.py:273
  41.4 9.6 %all_to_all.16.got_ref = f32[16,8,128]{2,1,0:T(8,128)S(1)} all-to-all(f32[16,8,128]{2,1,0:T(8,128)S(1)} %get-tuple-element.21), channel_id=1, replica_groups=mesh['parts'=2,'tensor'=16] {'tensor'}, dimensions={0} | all-to-all | bytes 131072 | tf_op jit(solution)/shard_map/all_to_all | solution.py:369
  51.1 11.9 %shard_map.122 = (f32[2,8,8192]{2,1,0:T(8,128)S(1)}, bf16[2,8,8192]{2,1,0:T(8,128)(2,1)S(1)}, bf16[16,1024]{1,0:T(8,128)(2,1)S(1)}, bf16[32,64]{1,0:T(8,128)(2,1)S(1)}) custom-call(f32[16,8,128]{2,1,0:T(8,128)S(1)} %all_to_all.16.got_ref, f32[16,1]{1,0:T(8,128)S(1)} %slice_add_fusion.slot_ref, f32[16,1024]{1,0:T(8,128)S(1)} %get-tuple-element.22.gate_ref, ...), custom_call_target="tpu_custom_call" | custom-call | tf_op jit(solution)/shard_map/pallas_call | solution.py:273
  63.0 0.1 collective-permute-start.1
  63.1 1.5 %collective-permute-done.1.got_ref = bf16[2,8,8192]{2,1,0:T(8,128)(2,1)S(1)} collective-permute-done((bf16[2,8,8192]{2,1,0:T(8,128)(2,1)S(1)}, bf16[2,8,8192]{2,1,0:T(8,128)(2,1)S(1)}, u32[]{:S(2)}, u32[]{:S(2)}) %collective-permute-start.1) | collective-permute-done | bytes 262176 | tf_op jit(solution)/shard_map/ppermute | solution.py:385
  64.6 0.8 %shard_map.123 = bf16[8,2,8192]{2,1,0:T(2,128)(2,1)} custom-call(f32[2,8,8192]{2,1,0:T(8,128)S(1)} %get-tuple-element.29.own_ref, bf16[2,8,8192]{2,1,0:T(8,128)(2,1)S(1)} %collective-permute-done.1.got_ref), custom_call_target="tpu_custom_call" | custom-call | tf_op jit(solution)/shard_map/pallas_call | solution.py:273
  65.4 3.4 %all-to-all-start.2 = ((bf16[8,2,8192]{2,1,0:T(2,128)(2,1)}), bf16[8,2,8192]{2,1,0:T(2,128)(2,1)S(1)}, u32[]{:S(2)}, u32[]{:S(2)}) async-start(bf16[8,2,8192]{2,1,0:T(2,128)(2,1)} %shard_map.123), calls=%async_computation.2 | async-start | bytes 524288 | tf_op jit(solution)/shard_map/all_to_all | solution.py:389
  68.8 2.7 %shard_map.125 = (bf16[1024,1024]{1,0:T(8,128)(2,1)}, bf16[64,8192]{1,0:T(8,128)(2,1)}) custom-call(bf16[16,1024]{1,0:T(8,128)(2,1)S(1)} %get-tuple-element.33.left_ref, bf16[16,1024]{1,0:T(8,128)(2,1)S(1)} %get-tuple-element.34.hid_ref, bf16[32,64]{1,0:T(8,128)(2,1)S(1)} %get-tuple-element.35.weighted_ref, bf16[16,8192]{1,0:T(8,128)(2,1)S(1)} %get-tuple-element.38.c_ref), custom_call_target="tpu_custom_call" | custom-call | flops 33554432 | bytes 3145728 | tf_op jit(solution)/shard_map/pallas_call | solution.py:273
  71.6 6.7 %all-to-all-done.2.back_ref = bf16[8,2,8192]{2,1,0:T(2,128)(2,1)S(1)} async-done(((bf16[8,2,8192]{2,1,0:T(2,128)(2,1)}), bf16[8,2,8192]{2,1,0:T(2,128)(2,1)S(1)}, u32[]{:S(2)}, u32[]{:S(2)}) %all-to-all-start.2) | async-done | bytes 262176 | tf_op jit(solution)/shard_map/all_to_all | solution.py:389
  78.3 0.9 %shard_map.124 = (bf16[1,8192]{1,0:T(2,128)(2,1)}, bf16[1,8192]{1,0:T(2,128)(2,1)}) custom-call(bf16[8,2,8192]{2,1,0:T(2,128)(2,1)S(1)} %all-to-all-done.2.back_ref), custom_call_target="tpu_custom_call" | custom-call | tf_op jit(solution)/shard_map/pallas_call | solution.py:273
  (4 shorter events, 0.1 us)
Async XLA Ops:
  19.0 1.6 %collective-permute-start = (bf16[8,2,8320]{2,0,1:T(8,128)(2,1)S(1)}, bf16[8,2,8320]{2,0,1:T(8,128)(2,1)S(1)}, u32[]{:S(2)}, u32[]{:S(2)}) collective-permute-start(bf16[8,2,8320]{2,0,1:T(8,128)(2,1)S(1)} %get-tuple-element.40), channel_id=1, source_target_pairs={{0,1},{1,0},{2,3},{3,2},{4,5},{5,4},{6,7},{7,6},{8,9},{9,8},{10,11... | collective-permute-start | bytes 798728 | tf_op jit(solution)/shard_map/ppermute | solution.py:336
  63.0 1.6 %collective-permute-start.1 = (bf16[2,8,8192]{2,1,0:T(8,128)(2,1)S(1)}, bf16[2,8,8192]{2,1,0:T(8,128)(2,1)S(1)}, u32[]{:S(2)}, u32[]{:S(2)}) collective-permute-start(bf16[2,8,8192]{2,1,0:T(8,128)(2,1)S(1)} %get-tuple-element.30), channel_id=1, source_target_pairs={{0,1},{1,0},{2,3},{3,2},{4,5},{5,4},{6,7},{7,6},{8,9},{9,8},{10,11... | collective-permute-start | bytes 786440 | tf_op jit(solution)/shard_map/ppermute | solution.py:385
  65.4 12.9 %all-to-all-start.2 = ((bf16[8,2,8192]{2,1,0:T(2,128)(2,1)}), bf16[8,2,8192]{2,1,0:T(2,128)(2,1)S(1)}, u32[]{:S(2)}, u32[]{:S(2)}) async-start(bf16[8,2,8192]{2,1,0:T(2,128)(2,1)} %shard_map.123), calls=%async_computation.2 | async-start | bytes 524288 | tf_op jit(solution)/shard_map/all_to_all | solution.py:389

commit v5 on v3

--- a/solution.py
+++ b/solution.py
@@ -93,16 +93,15 @@
         m.start()
     for m in moves:
         m.wait()
-    width = tokens_ref.shape[1]
     slot = table_ref[index_ref[0]]
-    lane = lax.broadcasted_iota(jnp.int32, (1, SPLIT), 1)
+    lane = lax.broadcasted_iota(jnp.int32, (2, SPLIT), 1)
     digits = jnp.where(lane == 0, slot // SPLIT, jnp.where(lane == 1, slot % SPLIT, 0))
-    digits = digits.astype(f32).astype(bf16)
+    rows = jnp.concatenate(
+        (tokens_ref[...].astype(f32), cotangent_ref[...].astype(f32)), axis=0
+    )
+    rows = jnp.concatenate((rows, digits.astype(f32)), axis=1).astype(bf16)
     for i in range(out_ref.shape[0]):
-        out_ref[i, 0:1, :width] = tokens_ref[...]
-        out_ref[i, 1:2, :width] = cotangent_ref[...]
-        out_ref[i, 0:1, width:] = digits
-        out_ref[i, 1:2, width:] = digits
+        out_ref[i] = rows
 
 
 def blocks(size, step):

time: 79.8 us -> 79.8 us (level)
  no operation moved by 1% of the time
where the time goes in v5:
time: 79.8 us; the launch traced here: 79.4 us
  Pallas kernels  36.1 us (45%)
  blocking collectives  26.5 us (33%)
  waiting for transfers between devices  9.76 us (12%)
  starting transfers between devices  3.55 us (4%)
  local copies, waits for them, and re-layouts  1.74 us (2%)
  between operations  1.35 us (2%)
    pallas_call x4, Pallas kernels, call(): pl.pallas_call(kernel, in_specs=specs or [VMEM] * len(args), out_specs=ou...  36.1 us
    all_to_all x1, blocking collectives, per_device(): lax.all_to_all(sent, 'tensor', 0, 0, axis_index_groups=same_core, tiled=T...  16.9 us
    all_to_all x1, blocking collectives, per_device(): got = lax.all_to_all(pay, 'tensor', 0, 0)  9.64 us
    all_to_all x1, waiting for transfers between devices, per_device(): lax.all_to_all(summed, 'tensor', 0, 0, axis_index_groups=same_core, tiled...  6.71 us
    all_to_all x1, starting transfers between devices, per_device(): lax.all_to_all(summed, 'tensor', 0, 0, axis_index_groups=same_core, tiled...  3.41 us
  transfers between devices with their start and end apart: 3, of which 3 were waited for; matrix products, arithmetic and copies ran while one was open for 0% of the time, Pallas kernels for 3%

profile of v5, /device:TPU:0, one launch (start us, length us, event | category | flops | bytes accessed | tf_op | source)
XLA Modules:
  0.0 79.4 jit_solution(8919100217522641927)
XLA Ops:
  1.3 0.9 %shard_map.120 = bf16[8,2,8320]{2,1,0:T(2,128)(2,1)S(1)} custom-call(s32[1]{0:T(128)S(6)} %copy.33.index_ref, s32[64]{0:T(128)} %table_hbm.1, bf16[1,8192]{1,0:T(2,128)(2,1)} %tokens_hbm.1, bf16[1,8192]{1,0:T(2,128)(2,1)} %cotangent_hbm.1), custom_call_target="tpu_custom_call" | custom-call | tf_op jit(solution)/shard_map/pallas_call | solution.py:259
  2.1 16.9 %all_to_all.15 = bf16[8,2,8320]{2,1,0:T(2,128)(2,1)S(1)} all-to-all(bf16[8,2,8320]{2,1,0:T(2,128)(2,1)S(1)} %shard_map.120), channel_id=1, replica_groups={{0,2,4,6,8,10,12,14},{1,3,5,7,9,11,13,15},{16,18,20,22,24,26,28,30},{17..., dimensions={0} | all-to-all | bytes 532480 | tf_op jit(solution)/shard_map/all_to_all | solution.py:321
  19.0 0.1 collective-permute-start
  19.1 1.5 %collective-permute-done = bf16[8,2,8320]{2,0,1:T(8,128)(2,1)S(1)} collective-permute-done((bf16[8,2,8320]{2,0,1:T(8,128)(2,1)S(1)}, bf16[8,2,8320]{2,0,1:T(8,128)(2,1)S(1)}, u32[]{:S(2)}, u32[]{:S(2)}) %collective-permute-start) | collective-permute-done | bytes 266272 | tf_op jit(solution)/shard_map/ppermute | solution.py:322
  20.7 0.1 slice_add_fusion.slot_ref
  20.8 20.6 %shard_map.121 = (f32[16,1024]{1,0:T(8,128)S(1)}, f32[16,1024]{1,0:T(8,128)S(1)}, bf16[16,1024]{1,0:T(8,128)(2,1)S(1)}, f32[16,8,128]{2,1,0:T(8,128)S(1)}, f32[1...) custom-call(bf16[16,8192]{1,0:T(8,128)(2,1)S(1)} %get-tuple-element., ...), custom_call_target="tpu_custom_call" | custom-call | tf_op jit(solution)/shard_map/pallas_call | solution.py:259
  41.4 9.6 %all_to_all.16.got_ref = f32[16,8,128]{2,1,0:T(8,128)S(1)} all-to-all(f32[16,8,128]{2,1,0:T(8,128)S(1)} %get-tuple-element.19), channel_id=1, replica_groups=mesh['parts'=2,'tensor'=16] {'tensor'}, dimensions={0} | all-to-all | bytes 131072 | tf_op jit(solution)/shard_map/all_to_all | solution.py:355
  51.1 11.9 %shard_map.122 = (f32[2,8,8192]{2,1,0:T(8,128)S(1)}, bf16[2,8,8192]{2,1,0:T(8,128)(2,1)S(1)}, bf16[16,1024]{1,0:T(8,128)(2,1)S(1)}, bf16[32,64]{1,0:T(8,128)(2,1)S(1)}) custom-call(f32[16,8,128]{2,1,0:T(8,128)S(1)} %all_to_all.16.got_ref, f32[16,1]{1,0:T(8,128)S(1)} %slice_add_fusion.slot_ref, f32[16,1024]{1,0:T(8,128)S(1)} %get-tuple-element.20.gate_ref, ...), custom_call_target="tpu_custom_call" | custom-call | tf_op jit(solution)/shard_map/pallas_call | solution.py:259
  63.0 0.1 collective-permute-start.1
  63.1 1.5 %collective-permute-done.1 = bf16[2,8,8192]{2,1,0:T(8,128)(2,1)S(1)} collective-permute-done((bf16[2,8,8192]{2,1,0:T(8,128)(2,1)S(1)}, bf16[2,8,8192]{2,1,0:T(8,128)(2,1)S(1)}, u32[]{:S(2)}, u32[]{:S(2)}) %collective-permute-start.1) | collective-permute-done | bytes 262176 | tf_op jit(solution)/shard_map/ppermute | solution.py:369
  64.6 1.0 %copy.28 = bf16[8,2,8192]{2,1,0:T(2,128)(2,1)} copy(bf16[8,2,8192]{2,0,1:T(8,128)(2,1)S(1)} %fusion) | data formatting | bytes 524288 | tf_op jit(solution)/shard_map/reshape | solution.py:372
  65.6 3.4 %all-to-all-start.2 = ((bf16[8,2,8192]{2,1,0:T(2,128)(2,1)}), bf16[8,2,8192]{2,1,0:T(2,128)(2,1)S(1)}, u32[]{:S(2)}, u32[]{:S(2)}) async-start(bf16[8,2,8192]{2,1,0:T(2,128)(2,1)} %copy.28), calls=%async_computation.2 | async-start | bytes 524288 | tf_op jit(solution)/shard_map/all_to_all | solution.py:373
  69.0 2.7 %shard_map.123 = (bf16[1024,1024]{1,0:T(8,128)(2,1)}, bf16[64,8192]{1,0:T(8,128)(2,1)}) custom-call(bf16[16,1024]{1,0:T(8,128)(2,1)S(1)} %get-tuple-element.29.left_ref, bf16[16,1024]{1,0:T(8,128)(2,1)S(1)} %get-tuple-element.30.hid_ref, bf16[32,64]{1,0:T(8,128)(2,1)S(1)} %get-tuple-element.31.weighted_ref, bf16[16,8192]{1,0:T(8,128)(2,1)S(1)} %get-tuple-element.34.c_ref), custom_call_target="tpu_custom_call" | custom-call | flops 33554432 | bytes 3145728 | tf_op jit(solution)/shard_map/pallas_call | solution.py:259
  71.7 6.7 %all-to-all-done.2 = bf16[8,2,8192]{2,1,0:T(2,128)(2,1)S(1)} async-done(((bf16[8,2,8192]{2,1,0:T(2,128)(2,1)}), bf16[8,2,8192]{2,1,0:T(2,128)(2,1)S(1)}, u32[]{:S(2)}, u32[]{:S(2)}) %all-to-all-start.2) | async-done | bytes 262176 | tf_op jit(solution)/shard_map/all_to_all | solution.py:373
  78.5 0.2 reduce_sum.12
  78.7 0.7 fusion.3
  (5 shorter events, 0.2 us)
Async XLA Ops:
  19.0 1.6 %collective-permute-start = (bf16[8,2,8320]{2,0,1:T(8,128)(2,1)S(1)}, bf16[8,2,8320]{2,0,1:T(8,128)(2,1)S(1)}, u32[]{:S(2)}, u32[]{:S(2)}) collective-permute-start(bf16[8,2,8320]{2,0,1:T(8,128)(2,1)S(1)} %get-tuple-element.36), channel_id=1, source_target_pairs={{0,1},{1,0},{2,3},{3,2},{4,5},{5,4},{6,7},{7,6},{8,9},{9,8},{10,11... | collective-permute-start | bytes 798728 | tf_op jit(solution)/shard_map/ppermute | solution.py:322
  63.0 1.6 %collective-permute-start.1 = (bf16[2,8,8192]{2,1,0:T(8,128)(2,1)S(1)}, bf16[2,8,8192]{2,1,0:T(8,128)(2,1)S(1)}, u32[]{:S(2)}, u32[]{:S(2)}) collective-permute-start(bf16[2,8,8192]{2,1,0:T(8,128)(2,1)S(1)} %get-tuple-element.28), channel_id=1, source_target_pairs={{0,1},{1,0},{2,3},{3,2},{4,5},{5,4},{6,7},{7,6},{8,9},{9,8},{10,11... | collective-permute-start | bytes 786440 | tf_op jit(solution)/shard_map/ppermute | solution.py:369
  65.6 12.9 %all-to-all-start.2 = ((bf16[8,2,8192]{2,1,0:T(2,128)(2,1)}), bf16[8,2,8192]{2,1,0:T(2,128)(2,1)S(1)}, u32[]{:S(2)}, u32[]{:S(2)}) async-start(bf16[8,2,8192]{2,1,0:T(2,128)(2,1)} %copy.28), calls=%async_computation.2 | async-start | bytes 524288 | tf_op jit(solution)/shard_map/all_to_all | solution.py:373

commit v6 on v4

--- a/solution.py
+++ b/solution.py
@@ -194,7 +194,7 @@
     total, hidden_dev = gate_ref.shape
     width = wg_ref.shape[0]
     piece = fit(width, 1024)
-    stream = Stream(AHEAD)
+    stream = Stream(2)
     for j, k in enumerate(blocks(width, piece)):
         stream.add(wu_hbm.at[k], wu_ref.at[k], su.at[j])
     stream.fill()
@@ -226,14 +226,14 @@
     high = jnp.where(mine, dot(high, fold), 0.0).astype(bf16)
     low = jnp.where(mine, dot(low, fold), 0.0).astype(bf16)
     weighted_ref[...] = jnp.concatenate((high, low), axis=0)
-    for s in blocks(width, 2 * piece):
+    for s in blocks(width, piece):
         us = u_ref[:, s]
         adapted = adapter_scale * (dot(high, us) + dot(low, us))
         out = base_ref[:, s] + adapted.astype(bf16).astype(f32)
         own_ref[0, :, s] = out[:half]
         sib_ref[0, :, s] = out[half:].astype(bf16)
-        stream.take(2)
-        for i in range(8):
+        stream.take()
+        for i in range(4):
             t = pl.ds(s.start + i * piece // 4, piece // 4)
             inp = dot(gg, wg_ref[t, :], NT) + dot(gu, wu_ref[t, :], NT)
             own_ref[1, :, t] = inp[:half]

time: 79.5 us -> 79.9 us (level)
  no operation moved by 1% of the time
where the time goes in v6:
time: 79.9 us; the launch traced here: 79.6 us
  Pallas kernels  38.2 us (48%)
  blocking collectives  26.5 us (33%)
  waiting for transfers between devices  9.76 us (12%)
  starting transfers between devices  3.55 us (4%)
  between operations  1.35 us (2%)
    pallas_call x6, Pallas kernels, call(): pl.pallas_call(kernel, in_specs=specs or [VMEM] * len(args), out_specs=ou...  38.2 us
    all_to_all x1, blocking collectives, per_device(): lax.all_to_all(sent, 'tensor', 0, 0, axis_index_groups=same_core, tiled=T...  16.9 us
    all_to_all x1, blocking collectives, per_device(): got = lax.all_to_all(pay, 'tensor', 0, 0)  9.64 us
    all_to_all x1, waiting for transfers between devices, per_device(): lax.all_to_all(summed, 'tensor', 0, 0, axis_index_groups=same_core, tiled...  6.71 us
    all_to_all x1, starting transfers between devices, per_device(): lax.all_to_all(summed, 'tensor', 0, 0, axis_index_groups=same_core, tiled...  3.41 us
  transfers between devices with their start and end apart: 3, of which 3 were waited for; matrix products, arithmetic and copies ran while one was open for 0% of the time, Pallas kernels for 3%

profile of v6, /device:TPU:0, one launch (start us, length us, event | category | flops | bytes accessed | tf_op | source)
XLA Modules:
  0.0 79.6 jit_solution(3017861127303630627)
XLA Ops:
  1.3 0.9 %shard_map.120 = bf16[8,2,8320]{2,1,0:T(2,128)(2,1)S(1)} custom-call(s32[1]{0:T(128)S(6)} %copy.31.index_ref, s32[64]{0:T(128)} %table_hbm.1, bf16[1,8192]{1,0:T(2,128)(2,1)} %tokens_hbm.1, bf16[1,8192]{1,0:T(2,128)(2,1)} %cotangent_hbm.1), custom_call_target="tpu_custom_call" | custom-call | tf_op jit(solution)/shard_map/pallas_call | solution.py:273
  2.1 16.9 %all_to_all.15 = bf16[8,2,8320]{2,1,0:T(2,128)(2,1)S(1)} all-to-all(bf16[8,2,8320]{2,1,0:T(2,128)(2,1)S(1)} %shard_map.120), channel_id=1, replica_groups={{0,2,4,6,8,10,12,14},{1,3,5,7,9,11,13,15},{16,18,20,22,24,26,28,30},{17..., dimensions={0} | all-to-all | bytes 532480 | tf_op jit(solution)/shard_map/all_to_all | solution.py:335
  19.0 0.1 collective-permute-start
  19.1 1.5 %collective-permute-done = bf16[8,2,8320]{2,0,1:T(8,128)(2,1)S(1)} collective-permute-done((bf16[8,2,8320]{2,0,1:T(8,128)(2,1)S(1)}, bf16[8,2,8320]{2,0,1:T(8,128)(2,1)S(1)}, u32[]{:S(2)}, u32[]{:S(2)}) %collective-permute-start) | collective-permute-done | bytes 266272 | tf_op jit(solution)/shard_map/ppermute | solution.py:336
  20.7 0.1 slice_add_fusion.slot_ref
  20.8 20.6 %shard_map.121 = (f32[16,1024]{1,0:T(8,128)S(1)}, f32[16,1024]{1,0:T(8,128)S(1)}, bf16[16,1024]{1,0:T(8,128)(2,1)S(1)}, f32[16,8,128]{2,1,0:T(8,128)S(1)}, f32[1...) custom-call(bf16[16,8192]{1,0:T(8,128)(2,1)S(1)} %get-tuple-element., ...), custom_call_target="tpu_custom_call" | custom-call | tf_op jit(solution)/shard_map/pallas_call | solution.py:273
  41.4 9.6 %all_to_all.16.got_ref = f32[16,8,128]{2,1,0:T(8,128)S(1)} all-to-all(f32[16,8,128]{2,1,0:T(8,128)S(1)} %get-tuple-element.21), channel_id=1, replica_groups=mesh['parts'=2,'tensor'=16] {'tensor'}, dimensions={0} | all-to-all | bytes 131072 | tf_op jit(solution)/shard_map/all_to_all | solution.py:369
  51.1 12.3 %shard_map.122 = (f32[2,8,8192]{2,1,0:T(8,128)S(1)}, bf16[2,8,8192]{2,1,0:T(8,128)(2,1)S(1)}, bf16[16,1024]{1,0:T(8,128)(2,1)S(1)}, bf16[32,64]{1,0:T(8,128)(2,1)S(1)}) custom-call(f32[16,8,128]{2,1,0:T(8,128)S(1)} %all_to_all.16.got_ref, f32[16,1]{1,0:T(8,128)S(1)} %slice_add_fusion.slot_ref, f32[16,1024]{1,0:T(8,128)S(1)} %get-tuple-element.22.gate_ref, ...), custom_call_target="tpu_custom_call" | custom-call | tf_op jit(solution)/shard_map/pallas_call | solution.py:273
  63.4 0.1 collective-permute-start.1
  63.4 1.5 %collective-permute-done.1.got_ref = bf16[2,8,8192]{2,1,0:T(8,128)(2,1)S(1)} collective-permute-done((bf16[2,8,8192]{2,1,0:T(8,128)(2,1)S(1)}, bf16[2,8,8192]{2,1,0:T(8,128)(2,1)S(1)}, u32[]{:S(2)}, u32[]{:S(2)}) %collective-permute-start.1) | collective-permute-done | bytes 262176 | tf_op jit(solution)/shard_map/ppermute | solution.py:385
  65.0 0.8 %shard_map.123 = bf16[8,2,8192]{2,1,0:T(2,128)(2,1)} custom-call(f32[2,8,8192]{2,1,0:T(8,128)S(1)} %get-tuple-element.29.own_ref, bf16[2,8,8192]{2,1,0:T(8,128)(2,1)S(1)} %collective-permute-done.1.got_ref), custom_call_target="tpu_custom_call" | custom-call | tf_op jit(solution)/shard_map/pallas_call | solution.py:273
  65.8 3.4 %all-to-all-start.2 = ((bf16[8,2,8192]{2,1,0:T(2,128)(2,1)}), bf16[8,2,8192]{2,1,0:T(2,128)(2,1)S(1)}, u32[]{:S(2)}, u32[]{:S(2)}) async-start(bf16[8,2,8192]{2,1,0:T(2,128)(2,1)} %shard_map.123), calls=%async_computation.2 | async-start | bytes 524288 | tf_op jit(solution)/shard_map/all_to_all | solution.py:389
  69.2 2.7 %shard_map.125 = (bf16[1024,1024]{1,0:T(8,128)(2,1)}, bf16[64,8192]{1,0:T(8,128)(2,1)}) custom-call(bf16[16,1024]{1,0:T(8,128)(2,1)S(1)} %get-tuple-element.33.left_ref, bf16[16,1024]{1,0:T(8,128)(2,1)S(1)} %get-tuple-element.34.hid_ref, bf16[32,64]{1,0:T(8,128)(2,1)S(1)} %get-tuple-element.35.weighted_ref, bf16[16,8192]{1,0:T(8,128)(2,1)S(1)} %get-tuple-element.38.c_ref), custom_call_target="tpu_custom_call" | custom-call | flops 33554432 | bytes 3145728 | tf_op jit(solution)/shard_map/pallas_call | solution.py:273
  72.0 6.7 %all-to-all-done.2.back_ref = bf16[8,2,8192]{2,1,0:T(2,128)(2,1)S(1)} async-done(((bf16[8,2,8192]{2,1,0:T(2,128)(2,1)}), bf16[8,2,8192]{2,1,0:T(2,128)(2,1)S(1)}, u32[]{:S(2)}, u32[]{:S(2)}) %all-to-all-start.2) | async-done | bytes 262176 | tf_op jit(solution)/shard_map/all_to_all | solution.py:389
  78.7 0.9 %shard_map.124 = (bf16[1,8192]{1,0:T(2,128)(2,1)}, bf16[1,8192]{1,0:T(2,128)(2,1)}) custom-call(bf16[8,2,8192]{2,1,0:T(2,128)(2,1)S(1)} %all-to-all-done.2.back_ref), custom_call_target="tpu_custom_call" | custom-call | tf_op jit(solution)/shard_map/pallas_call | solution.py:273
  (4 shorter events, 0.1 us)
Async XLA Ops:
  19.0 1.6 %collective-permute-start = (bf16[8,2,8320]{2,0,1:T(8,128)(2,1)S(1)}, bf16[8,2,8320]{2,0,1:T(8,128)(2,1)S(1)}, u32[]{:S(2)}, u32[]{:S(2)}) collective-permute-start(bf16[8,2,8320]{2,0,1:T(8,128)(2,1)S(1)} %get-tuple-element.40), channel_id=1, source_target_pairs={{0,1},{1,0},{2,3},{3,2},{4,5},{5,4},{6,7},{7,6},{8,9},{9,8},{10,11... | collective-permute-start | bytes 798728 | tf_op jit(solution)/shard_map/ppermute | solution.py:336
  63.4 1.6 %collective-permute-start.1 = (bf16[2,8,8192]{2,1,0:T(8,128)(2,1)S(1)}, bf16[2,8,8192]{2,1,0:T(8,128)(2,1)S(1)}, u32[]{:S(2)}, u32[]{:S(2)}) collective-permute-start(bf16[2,8,8192]{2,1,0:T(8,128)(2,1)S(1)} %get-tuple-element.30), channel_id=1, source_target_pairs={{0,1},{1,0},{2,3},{3,2},{4,5},{5,4},{6,7},{7,6},{8,9},{9,8},{10,11... | collective-permute-start | bytes 786440 | tf_op jit(solution)/shard_map/ppermute | solution.py:385
  65.8 12.9 %all-to-all-start.2 = ((bf16[8,2,8192]{2,1,0:T(2,128)(2,1)}), bf16[8,2,8192]{2,1,0:T(2,128)(2,1)S(1)}, u32[]{:S(2)}, u32[]{:S(2)}) async-start(bf16[8,2,8192]{2,1,0:T(2,128)(2,1)} %shard_map.123), calls=%async_computation.2 | async-start | bytes 524288 | tf_op jit(solution)/shard_map/all_to_all | solution.py:389
